TPU v7x, 256 devices: a whole 4x4x8 slice. The times are simulated.
256 devices in a mesh: gx: 64 (over z, x, y_hi), gy: 4 (over y_lo, core).
Axes of the slice: x: 4, y: 4 (y_hi: 2, y_lo: 2; y = y_hi * 2 + y_lo), z: 8, core: 2. Of those that a mesh axis runs over, the one named last changes fastest.
Arguments:
- charges: float32 [1536, 256, 128], P('gx', 'gy'), may hold values from -4 to 4
- kernel_fine: bfloat16 [15, 15, 15], replicated, may hold values from 0 to 1
- kernel_mid: bfloat16 [15, 15, 15], replicated, may hold values from 0 to 1
- kernel_top: bfloat16 [15, 15, 15], replicated, may hold values from 0 to 1
Outputs:
- potential: float32 [1536, 256, 128], P('gx', 'gy')
All inputs are finite; a program needn't handle non-finite values.
Results may differ from a plain program's by a relative error of at most 0.0035.
Values may be sent and summed in bfloat16 or wider, within the bound.
A program may use at most 256 MiB of HBM per device.

v0:
```python
import jax
import jax.numpy as jnp
from jax import lax
from jax.sharding import PartitionSpec as P


def from_behind(value, axis, by):
    length = lax.axis_size(axis)
    pairs = [(i, i + by) for i in range(length) if 0 <= i + by < length]
    return lax.ppermute(value, axis, pairs)


def padded(cells, sides, width):
    for axis, dim in sides:
        count = lax.axis_size(axis)
        ends = count - 1
        head = lax.slice_in_dim(cells, 0, width, axis=dim)
        tail = lax.slice_in_dim(cells, cells.shape[dim] - width, cells.shape[dim], axis=dim)
        cells = jnp.concatenate(
            [
                lax.ppermute(tail, axis, [(i, (i + 1) % count) for i in range(ends)]),
                cells,
                lax.ppermute(head, axis, [((i + 1) % count, i) for i in range(ends)]),
            ],
            axis=dim,
        )
    return cells


def restrict_axis(values, axis, count):
    left_part = lax.slice_in_dim(values, 0, 2 * count, 2, axis)
    middle_part = lax.slice_in_dim(values, 1, 2 * count, 2, axis)
    right_part = lax.slice_in_dim(values, 2, 2 * count + 1, 2, axis)
    return 0.5 * left_part + middle_part + 0.5 * right_part


def restrict(extended, start, count_x, count_y):
    layer_count = extended.shape[2]
    values = extended[start : start + 2 * count_x + 1, start : start + 2 * count_y + 1, :].astype(
        jnp.float32
    )
    values = jnp.pad(values, ((0, 0), (0, 0), (1, 0)))
    values = restrict_axis(values, 0, count_x)
    values = restrict_axis(values, 1, count_y)
    return restrict_axis(values, 2, layer_count // 2)


def prolong_axis(values, axis, count):
    first_part = lax.slice_in_dim(values, 0, count, 1, axis)
    second_part = lax.slice_in_dim(values, 1, count + 1, 1, axis)
    middle_part = 0.5 * (first_part + second_part)
    joined = jnp.stack((first_part, middle_part), axis=axis + 1)
    new_shape = list(values.shape)
    new_shape[axis] = 2 * count
    return joined.reshape(new_shape)


def interpolate(coarse):
    count_x, count_y, layer_count = coarse.shape
    next_row = from_behind(coarse[:1], "gx", -1)
    widened = jnp.concatenate((coarse, next_row), axis=0)
    next_column = from_behind(widened[:, :1], "gy", -1)
    widened = jnp.concatenate((widened, next_column), axis=1)
    widened = jnp.pad(widened, ((0, 0), (0, 0), (0, 1)))
    widened = prolong_axis(widened, 0, count_x)
    widened = prolong_axis(widened, 1, count_y)
    return prolong_axis(widened, 2, layer_count)


def with_margin(field):
    return padded(field, (("gx", 0), ("gy", 1)), 7)


def correlate(extended, kernel):
    row_count = extended.shape[0] - 14
    col_count = extended.shape[1] - 14
    layer_count = extended.shape[2]
    tile_width = min(max(1, 256 // layer_count), col_count)
    block_count = col_count // tile_width
    span_width = tile_width + 14
    stacked = jnp.stack(
        [
            lax.slice_in_dim(
                extended, column, column + tile_width * (block_count - 1) + 1, tile_width, 1
            )
            for column in range(span_width)
        ],
        axis=2,
    )
    stacked = stacked.reshape(row_count + 14, block_count, span_width * layer_count)
    offsets = jnp.arange(15)
    pick_y = (
        jnp.arange(span_width)[None, :, None] - jnp.arange(tile_width)[None, None, :]
        == offsets[:, None, None]
    ).astype(jnp.bfloat16)
    pick_z = (
        jnp.arange(layer_count)[None, :, None] - jnp.arange(layer_count)[None, None, :] + 7
        == offsets[:, None, None]
    ).astype(jnp.bfloat16)
    partial_z = jnp.einsum("abc,cwz->abwz", kernel, pick_z)
    weights_all = jnp.einsum("abwz,bji->ajwiz", partial_z, pick_y)
    weights_all = weights_all.reshape(15, span_width * layer_count, tile_width * layer_count)

    def accumulate(offset_x, total):
        weights = lax.dynamic_index_in_dim(weights_all, offset_x, 0, keepdims=False)
        window = lax.dynamic_slice_in_dim(stacked, offset_x, row_count, 0)
        window = window.reshape(row_count * block_count, span_width * layer_count)
        return total + jnp.dot(window, weights, preferred_element_type=jnp.float32)

    initial = jnp.zeros((row_count * block_count, tile_width * layer_count), jnp.float32)
    total = lax.fori_loop(0, 15, accumulate, initial)
    return total.reshape(row_count, block_count, tile_width, layer_count).reshape(
        row_count, col_count, layer_count
    )


def nearby_coarse(top_cells, quarter_x):
    side_ext = padded(top_cells, (("gy", 1),), 7)
    reach = (quarter_x + 6) // quarter_x
    distances = list(range(reach, 0, -1)) + list(range(-1, -reach - 1, -1))
    pieces = {}
    for distance in distances:
        pieces[distance] = from_behind(side_ext, "gx", distance)
    ordered = (
        [pieces[distance] for distance in range(reach, 0, -1)]
        + [side_ext]
        + [pieces[distance] for distance in range(-1, -reach - 1, -1)]
    )
    joined = jnp.concatenate(ordered, axis=0)
    return joined[reach * quarter_x - 7 : (reach + 1) * quarter_x + 7]


def shards(charges, kernel_fine, kernel_mid, kernel_top):
    size_x, size_y, layer_count = charges.shape
    half_x, half_y = (size_x // 2, size_y // 2)
    quarter_x, quarter_y = (size_x // 4, size_y // 4)
    fine_cells = charges.astype(jnp.bfloat16)
    fine_ext = with_margin(fine_cells)
    mid_cells = restrict(fine_ext, 6, half_x, half_y).astype(jnp.bfloat16)
    mid_ext = with_margin(mid_cells)
    top_cells = restrict(mid_ext, 6, quarter_x, quarter_y).astype(jnp.bfloat16)
    top_ext = nearby_coarse(top_cells, quarter_x)
    fine_pot = correlate(fine_ext, kernel_fine)
    mid_pot = correlate(mid_ext, kernel_mid)
    top_pot = correlate(top_ext, kernel_top)
    mid_total = mid_pot + interpolate(top_pot)
    return fine_pot + interpolate(mid_total)


def solution(mesh):
    placed = (P("gx", "gy", None), P(), P(), P())
    return jax.shard_map(
        shards, mesh=mesh, in_specs=placed, out_specs=P("gx", "gy", None), check_vma=False
    )
```

profile of v0, /device:TPU:127, one launch (start us, length us, event | category | flops | bytes accessed | tf_op | source)
XLA Modules:
  0.0 456.4 jit_solution(1230954244323694046)
XLA Ops:
  1.2 5.3 %collective-permute-start = (bf16[7,64,128]{2,1,0:T(8,128)(2,1)S(1)}, bf16[7,64,128]{2,1,0:T(8,128)(2,1)S(1)}, u32[]{:S(2)}, u32[]{:S(2)}) collective-permute-start(bf16[7,64,128]{2,1,0:T(8,128)(2,1)S(1)} %get-tuple-element.328), channel_id=1, source_target_pairs={{0,4},{4,8},{8,12},{12,16},{16,20},{20,24},{24,28},{28,32},{32,36}... | collective-permute-start | bytes 344072 | tf_op jit(solution)/shard_map/ppermute | solution.py:21
  8.6 12.0 %convolution_bitcast_fusion.2 = bf16[15,18,64,4,64]{4,1,2,0,3:T(8,128)(2,1)} fusion(s32[64,64]{1,0:T(8,128)S(1)} %subtract_add_fusion.1, bf16[15,15,15]{2,1,0:T(8,128)(2,1)} %param.12, s32[18,4]{0,1:T(4,128)S(1)} %iota_subtract_fusion.1), kind=kOutput, calls=%fused_computation.18 | convolution fusion | flops 160420928 | bytes 8870782 | tf_op jit(solution)/shard_map/abwz,bji->ajwiz/dot_general | solution.py:101
  20.6 10.6 %convolution_bitcast_fusion.1 = bf16[15,22,32,8,32]{4,1,2,0,3:T(8,128)(2,1)} fusion(s32[32,32]{1,0:T(8,128)S(1)} %subtract_add_fusion.2, bf16[15,15,15]{2,1,0:T(8,128)(2,1)S(1)} %copy-done.10, s32[22,8]{0,1:T(8,128)S(1)} %iota_subtract_fusion), kind=kOutput, calls=%fused_computation.17 | convolution fusion | flops 88030800 | bytes 5418270 | tf_op jit(solution)/shard_map/abwz,bji->ajwiz/dot_general | solution.py:101
  32.7 3.7 collective-permute-start.3
  36.4 9.1 %convolution_bitcast_fusion = bf16[15,16,128,2,128]{4,1,2,0,3:T(8,128)(2,1)} fusion(s32[128,128]{1,0:T(8,128)S(1)} %subtract_add_fusion, bf16[15,15,15]{2,1,0:T(8,128)(2,1)S(1)} %copy-done, s32[16,2]{0,1:T(2,128)S(1)} %iota_subtract_fusion.2), kind=kOutput, calls=%fused_computation.16 | convolution fusion | flops 346767840 | bytes 15801054 | tf_op jit(solution)/shard_map/abwz,bji->ajwiz/dot_general | solution.py:101
  45.4 29.2 %copy.51 = bf16[15,16,128,2,128]{4,3,2,1,0:T(2,128)(2,1)} copy(bf16[15,16,128,2,128]{4,1,2,0,3:T(8,128)(2,1)} %convolution_bitcast_fusion) | data formatting | bytes 31457280
  74.7 25.3 %reshape.181 = bf16[15,2048,256]{2,1,0:T(8,128)(2,1)} reshape(bf16[15,16,128,2,128]{4,3,2,1,0:T(2,128)(2,1)} %copy.51) | data formatting | bytes 31457280
  100.0 17.8 %copy.30 = bf16[15,18,64,4,64]{4,3,2,1,0:T(4,128)(2,1)} copy(bf16[15,18,64,4,64]{4,1,2,0,3:T(8,128)(2,1)} %convolution_bitcast_fusion.2) | data formatting | bytes 17694720 | tf_op jit(solution)/shard_map/abwz,bji->ajwiz/transpose | solution.py:101
  117.8 25.5 %reshape.157 = bf16[15,1152,256]{2,1,0:T(8,128)(2,1)} reshape(bf16[15,18,64,4,64]{4,3,2,1,0:T(4,128)(2,1)} %copy.30) | data formatting | bytes 17694720 | tf_op jit(solution)/shard_map/reshape | solution.py:102
  143.3 23.8 %copy.32 = bf16[15,22,32,8,32]{4,3,2,1,0:T(8,128)(2,1)} copy(bf16[15,22,32,8,32]{4,1,2,0,3:T(8,128)(2,1)} %convolution_bitcast_fusion.1) | data formatting | bytes 10813440 | tf_op jit(solution)/shard_map/abwz,bji->ajwiz/transpose | solution.py:101
  167.1 25.8 %reshape.159 = bf16[15,704,256]{2,1,0:T(8,128)(2,1)} reshape(bf16[15,22,32,8,32]{4,3,2,1,0:T(8,128)(2,1)} %copy.32) | data formatting | bytes 10813440 | tf_op jit(solution)/shard_map/reshape | solution.py:102
  193.0 2.2 slice.326
  195.2 2.2 slice.325
  198.5 2.2 slice.331
  215.7 2.2 slice.321
  226.0 3.7 slice.343
  229.7 3.5 slice.342
  233.2 4.0 slice.341
  238.3 9.4 %collective-permute-start.4 = (bf16[7,32,64]{2,1,0:T(8,128)(2,1)S(1)}, bf16[7,32,64]{2,1,0:T(8,128)(2,1)S(1)}, u32[]{:S(2)}, u32[]{:S(2)}) collective-permute-start(bf16[7,32,64]{2,1,0:T(8,128)(2,1)S(1)} %get-tuple-element.338), channel_id=1, source_target_pairs={{0,4},{4,8},{8,12},{12,16},{16,20},{20,24},{24,28},{28,32},{32,36}... | collective-permute-start | bytes 86024 | tf_op jit(solution)/shard_map/ppermute | solution.py:21
  270.8 4.5 collective-permute-start.7
  279.6 4.3 collective-permute-start.9
  284.8 2.2 collective-permute-start.10
  287.1 3.1 collective-permute-start.13
  290.2 8.2 %collective-permute-start.12 = (bf16[6,30,32]{2,1,0:T(8,128)(2,1)S(1)}, bf16[6,30,32]{2,1,0:T(8,128)(2,1)S(1)}, u32[]{:S(2)}, u32[]{:S(2)}) collective-permute-start(bf16[6,30,32]{2,1,0:T(8,128)(2,1)S(1)} %pad_maximum_fusion.10), channel_id=1, source_target_pairs={{4,0},{8,4},{12,8},{16,12},{20,16},{24,20},{28,24},{32,28},{36,32}... | collective-permute-start | bytes 34568 | tf_op jit(solution)/shard_map/ppermute | solution.py:10
  298.4 6.4 %collective-permute-start.11 = (bf16[6,30,32]{2,1,0:T(8,128)(2,1)S(1)}, bf16[6,30,32]{2,1,0:T(8,128)(2,1)S(1)}, u32[]{:S(2)}, u32[]{:S(2)}) collective-permute-start(bf16[6,30,32]{2,1,0:T(8,128)(2,1)S(1)} %pad_maximum_fusion.10), channel_id=1, source_target_pairs={{0,4},{4,8},{8,12},{12,16},{16,20},{20,24},{24,28},{28,32},{32,36}... | collective-permute-start | bytes 34568 | tf_op jit(solution)/shard_map/ppermute | solution.py:10
  307.9 18.2 %while.44 = (s32[]{:T(128)}, f32[12,256]{1,0:T(8,128)S(1)}, bf16[20,2,704]{2,1,0:T(2,128)(2,1)S(1)}, bf16[15,704,256]{2,1,0:T(8,128)(2,1)}, s32[]{:T(128)}, /*index=5*/s32[]{:T(128)}) while((s32[]{:T(128)}, f32[12,256]{1,0:T(8,128)S(1)}, bf16[20,2,704]{2,1,0:T(2,128)(2,1)S(1)}, bf16[15,704,256]{2,1,0:T(8,128)(2,1)}, s32[]{:T(128)}, ...), condition=%wide.region_5.6_spmd.clone, body=%wide.region_4.5_spmd.clone.sunk | while | flops 4331523 | bytes 469599 | solution.py:111
  329.2 7.4 %collective-permute-done.14 = f32[1,16,32]{2,0,1:T(1,128)S(1)} collective-permute-done((f32[1,16,32]{2,0,1:T(1,128)S(1)}, f32[1,16,32]{2,0,1:T(1,128)S(1)}, u32[]{:S(2)}, u32[]{:S(2)}) %collective-permute-start.14) | collective-permute-done | bytes 2080 | tf_op jit(solution)/shard_map/ppermute | solution.py:10
  336.7 6.8 %collective-permute-start.15 = (f32[7,1,32]{2,0,1:T(8,128)S(1)}, f32[7,1,32]{2,0,1:T(8,128)S(1)}, u32[]{:S(2)}, u32[]{:S(2)}) collective-permute-start(f32[7,1,32]{2,0,1:T(8,128)S(1)} %pad_maximum_fusion.12), channel_id=1, source_target_pairs={{1,0},{2,1},{3,2},{5,4},{6,5},{7,6},{9,8},{10,9},{11,10},{13,12},{... | collective-permute-start | bytes 2696 | tf_op jit(solution)/shard_map/ppermute | solution.py:10
  343.5 20.4 %while.43 = (s32[]{:T(128)}, f32[96,256]{1,0:T(8,128)S(1)}, bf16[26,8,1152]{2,1,0:T(8,128)(2,1)S(1)}, bf16[15,1152,256]{2,1,0:T(8,128)(2,1)}, s32[]{:T(128)}, /*index=5*/s32[]{:T(128)}) while((s32[]{:T(128)}, f32[96,256]{1,0:T(8,128)S(1)}, bf16[26,8,1152]{2,1,0:T(8,128)(2,1)S(1)}, bf16[15,1152,256]{2,1,0:T(8,128)(2,1)}, s32[]{:T(128)}, ...), condition=%wide.region_3.4_spmd.clone, body=%wide.region_2.3_spmd.clone.sunk | while | flops 56672256 | bytes 1009238 | solution.py:111
  367.3 5.4 %copy_bitcast_fusion = bf16[38,32,2048]{2,1,0:T(8,128)(2,1)} fusion(bf16[38,32,16,128]{3,1,0,2:T(8,128)(2,1)} %bitcast_dynamic-update-slice_fusion), kind=kLoop, calls=%fused_computation.20 | loop fusion | bytes 9961472 | tf_op jit(solution)/shard_map/reshape | solution.py:90
  372.7 2.9 collective-permute-done.16
  375.6 3.1 collective-permute-start.17
  378.7 72.2 %while.42 = (s32[]{:T(128)}, f32[768,256]{1,0:T(8,128)S(1)}, bf16[38,32,2048]{2,1,0:T(8,128)(2,1)}, bf16[15,2048,256]{2,1,0:T(8,128)(2,1)}, s32[]{:T(128)}, /*index=5*/s32[]{:T(128)}) while((s32[]{:T(128)}, f32[768,256]{1,0:T(8,128)S(1)}, bf16[38,32,2048]{2,1,0:T(8,128)(2,1)}, bf16[15,2048,256]{2,1,0:T(8,128)(2,1)}, s32[]{:T(128)}, ...), condition=%wide.region_1.2_spmd.clone, body=%wide.region_0.1_spmd.clone.sunk | while | flops 805699584 | bytes 12058719 | solution.py:111
  378.7 2.3 constant_dynamic-slice_fusion.4
  381.0 2.5 convolution_add_fusion.6
  383.5 2.3 constant_dynamic-slice_fusion.4
  385.8 2.5 convolution_add_fusion.6
  388.3 2.3 constant_dynamic-slice_fusion.4
  390.6 2.5 convolution_add_fusion.6
  393.1 2.3 constant_dynamic-slice_fusion.4
  395.4 2.5 convolution_add_fusion.6
  397.9 2.3 constant_dynamic-slice_fusion.4
  400.2 2.5 convolution_add_fusion.6
  402.7 2.3 constant_dynamic-slice_fusion.4
  405.0 2.5 convolution_add_fusion.6
  407.5 2.3 constant_dynamic-slice_fusion.4
  409.8 2.5 convolution_add_fusion.6
  412.4 2.3 constant_dynamic-slice_fusion.4
  414.7 2.5 convolution_add_fusion.6
  417.2 2.3 constant_dynamic-slice_fusion.4
  419.5 2.5 convolution_add_fusion.6
  422.0 2.3 constant_dynamic-slice_fusion.4
  424.3 2.5 convolution_add_fusion.6
  426.8 2.3 constant_dynamic-slice_fusion.4
  429.1 2.5 convolution_add_fusion.6
  431.6 2.3 constant_dynamic-slice_fusion.4
  433.9 2.5 convolution_add_fusion.6
  436.4 2.3 constant_dynamic-slice_fusion.4
  438.7 2.5 convolution_add_fusion.6
  441.2 2.3 constant_dynamic-slice_fusion.4
  443.5 2.5 convolution_add_fusion.6
  446.0 2.3 constant_dynamic-slice_fusion.4
  448.4 2.5 convolution_add_fusion.6
  454.2 2.2 add.228
  (294 shorter events, 108.2 us)
Async XLA Ops:
  0.0 36.4 %copy-start = (bf16[15,15,15]{2,1,0:T(8,128)(2,1)S(1)}, bf16[15,15,15]{2,1,0:T(8,128)(2,1)}, u32[]{:S(2)}) copy-start(bf16[15,15,15]{2,1,0:T(8,128)(2,1)} %param.11) | copy-start | bytes 20254
  1.2 30.0 %collective-permute-start = (bf16[7,64,128]{2,1,0:T(8,128)(2,1)S(1)}, bf16[7,64,128]{2,1,0:T(8,128)(2,1)S(1)}, u32[]{:S(2)}, u32[]{:S(2)}) collective-permute-start(bf16[7,64,128]{2,1,0:T(8,128)(2,1)S(1)} %get-tuple-element.328), channel_id=1, source_target_pairs={{0,4},{4,8},{8,12},{12,16},{16,20},{20,24},{24,28},{28,32},{32,36}... | collective-permute-start | bytes 344072 | tf_op jit(solution)/shard_map/ppermute | solution.py:21
  6.6 24.7 %collective-permute-start.1 = (bf16[7,64,128]{2,1,0:T(8,128)(2,1)S(1)}, bf16[7,64,128]{2,1,0:T(8,128)(2,1)S(1)}, u32[]{:S(2)}, u32[]{:S(2)}) collective-permute-start(bf16[7,64,128]{2,1,0:T(8,128)(2,1)S(1)} %get-tuple-element.329), channel_id=1, source_target_pairs={{4,0},{8,4},{12,8},{16,12},{20,16},{24,20},{28,24},{32,28},{36,32}... | collective-permute-start | bytes 344072 | tf_op jit(solution)/shard_map/ppermute | solution.py:23
  8.6 12.0 %copy-start.10 = (bf16[15,15,15]{2,1,0:T(8,128)(2,1)S(1)}, bf16[15,15,15]{2,1,0:T(8,128)(2,1)}, u32[]{:S(2)}) copy-start(bf16[15,15,15]{2,1,0:T(8,128)(2,1)} %param.13) | copy-start | bytes 20254
  31.4 166.0 %collective-permute-start.2 = (bf16[38,7,128]{2,1,0:T(8,128)(2,1)S(1)}, bf16[38,7,128]{2,1,0:T(8,128)(2,1)S(1)}, u32[]{:S(2)}, u32[]{:S(2)}) collective-permute-start(bf16[38,7,128]{2,1,0:T(8,128)(2,1)S(1)} %get-tuple-element.324), channel_id=1, source_target_pairs={{0,1},{1,2},{2,3},{4,5},{5,6},{6,7},{8,9},{9,10},{10,11},{12,13},{... | collective-permute-start | bytes 204296 | tf_op jit(solution)/shard_map/ppermute | solution.py:21
  32.7 164.7 %collective-permute-start.3 = (bf16[38,7,128]{2,1,0:T(8,128)(2,1)S(1)}, bf16[38,7,128]{2,1,0:T(8,128)(2,1)S(1)}, u32[]{:S(2)}, u32[]{:S(2)}) collective-permute-start(bf16[38,7,128]{2,1,0:T(8,128)(2,1)S(1)} %get-tuple-element.325), channel_id=1, source_target_pairs={{1,0},{2,1},{3,2},{5,4},{6,5},{7,6},{9,8},{10,9},{11,10},{13,12},{... | collective-permute-start | bytes 204296 | tf_op jit(solution)/shard_map/ppermute | solution.py:23
  226.0 35.6 %copy-start.5 = (bf16[38,32,128]{2,1,0:T(8,128)(2,1)S(1)}, bf16[38,32,128]{2,1,0:T(8,128)(2,1)}, u32[]{:S(2)}) copy-start(bf16[38,32,128]{2,1,0:T(8,128)(2,1)} %slice.325) | copy-start | bytes 933892
  226.0 36.3 %copy-start.3 = (bf16[38,32,128]{2,1,0:T(8,128)(2,1)S(1)}, bf16[38,32,128]{2,1,0:T(8,128)(2,1)}, u32[]{:S(2)}) copy-start(bf16[38,32,128]{2,1,0:T(8,128)(2,1)} %slice.326) | copy-start | bytes 933892
  226.0 39.3 %copy-start.4 = (bf16[38,32,128]{2,1,0:T(8,128)(2,1)S(1)}, bf16[38,32,128]{2,1,0:T(8,128)(2,1)}, u32[]{:S(2)}) copy-start(bf16[38,32,128]{2,1,0:T(8,128)(2,1)} %slice.330) | copy-start | bytes 933892
  229.7 36.4 %copy-start.2 = (bf16[38,32,128]{2,1,0:T(8,128)(2,1)S(1)}, bf16[38,32,128]{2,1,0:T(8,128)(2,1)}, u32[]{:S(2)}) copy-start(bf16[38,32,128]{2,1,0:T(8,128)(2,1)} %slice.331) | copy-start | bytes 933892
  237.2 25.9 %copy-start.8 = (bf16[38,32,128]{2,1,0:T(8,128)(2,1)S(1)}, bf16[38,32,128]{2,1,0:T(8,128)(2,1)}, u32[]{:S(2)}) copy-start(bf16[38,32,128]{2,1,0:T(8,128)(2,1)} %slice.327) | copy-start | bytes 933892
  237.2 26.6 %copy-start.7 = (bf16[38,32,128]{2,1,0:T(8,128)(2,1)S(1)}, bf16[38,32,128]{2,1,0:T(8,128)(2,1)}, u32[]{:S(2)}) copy-start(bf16[38,32,128]{2,1,0:T(8,128)(2,1)} %slice.328) | copy-start | bytes 933892
  237.2 27.4 %copy-start.6 = (bf16[38,32,128]{2,1,0:T(8,128)(2,1)S(1)}, bf16[38,32,128]{2,1,0:T(8,128)(2,1)}, u32[]{:S(2)}) copy-start(bf16[38,32,128]{2,1,0:T(8,128)(2,1)} %slice.329) | copy-start | bytes 933892
  238.3 30.1 %collective-permute-start.4 = (bf16[7,32,64]{2,1,0:T(8,128)(2,1)S(1)}, bf16[7,32,64]{2,1,0:T(8,128)(2,1)S(1)}, u32[]{:S(2)}, u32[]{:S(2)}) collective-permute-start(bf16[7,32,64]{2,1,0:T(8,128)(2,1)S(1)} %get-tuple-element.338), channel_id=1, source_target_pairs={{0,4},{4,8},{8,12},{12,16},{16,20},{20,24},{24,28},{28,32},{32,36}... | collective-permute-start | bytes 86024 | tf_op jit(solution)/shard_map/ppermute | solution.py:21
  247.6 20.7 %collective-permute-start.5 = (bf16[7,32,64]{2,1,0:T(8,128)(2,1)S(1)}, bf16[7,32,64]{2,1,0:T(8,128)(2,1)S(1)}, u32[]{:S(2)}, u32[]{:S(2)}) collective-permute-start(bf16[7,32,64]{2,1,0:T(8,128)(2,1)S(1)} %get-tuple-element.339), channel_id=1, source_target_pairs={{4,0},{8,4},{12,8},{16,12},{20,16},{24,20},{28,24},{32,28},{36,32}... | collective-permute-start | bytes 86024 | tf_op jit(solution)/shard_map/ppermute | solution.py:23
  268.5 6.9 %collective-permute-start.6 = (bf16[26,7,64]{2,1,0:T(8,128)(2,1)S(1)}, bf16[26,7,64]{2,1,0:T(8,128)(2,1)S(1)}, u32[]{:S(2)}, u32[]{:S(2)}) collective-permute-start(bf16[26,7,64]{2,1,0:T(8,128)(2,1)S(1)} %get-tuple-element.332), channel_id=1, source_target_pairs={{0,1},{1,2},{2,3},{4,5},{5,6},{6,7},{8,9},{9,10},{10,11},{12,13},{... | collective-permute-start | bytes 69896 | tf_op jit(solution)/shard_map/ppermute | solution.py:21
  270.8 6.3 %collective-permute-start.7 = (bf16[26,7,64]{2,1,0:T(8,128)(2,1)S(1)}, bf16[26,7,64]{2,1,0:T(8,128)(2,1)S(1)}, u32[]{:S(2)}, u32[]{:S(2)}) collective-permute-start(bf16[26,7,64]{2,1,0:T(8,128)(2,1)S(1)} %get-tuple-element.333), channel_id=1, source_target_pairs={{1,0},{2,1},{3,2},{5,4},{6,5},{7,6},{9,8},{10,9},{11,10},{13,12},{... | collective-permute-start | bytes 69896 | tf_op jit(solution)/shard_map/ppermute | solution.py:23
  278.3 6.0 %collective-permute-start.8 = (bf16[6,7,32]{2,1,0:T(8,128)(2,1)S(1)}, bf16[6,7,32]{2,1,0:T(8,128)(2,1)S(1)}, u32[]{:S(2)}, u32[]{:S(2)}) collective-permute-start(bf16[6,7,32]{2,1,0:T(8,128)(2,1)S(1)} %get-tuple-element.342), channel_id=1, source_target_pairs={{0,1},{1,2},{2,3},{4,5},{5,6},{6,7},{8,9},{9,10},{10,11},{12,13},{... | collective-permute-start | bytes 8072 | tf_op jit(solution)/shard_map/ppermute | solution.py:21
  279.6 5.1 %collective-permute-start.9 = (bf16[6,7,32]{2,1,0:T(8,128)(2,1)S(1)}, bf16[6,7,32]{2,1,0:T(8,128)(2,1)S(1)}, u32[]{:S(2)}, u32[]{:S(2)}) collective-permute-start(bf16[6,7,32]{2,1,0:T(8,128)(2,1)S(1)} %get-tuple-element.343), channel_id=1, source_target_pairs={{1,0},{2,1},{3,2},{5,4},{6,5},{7,6},{9,8},{10,9},{11,10},{13,12},{... | collective-permute-start | bytes 8072 | tf_op jit(solution)/shard_map/ppermute | solution.py:23
  284.8 20.0 %collective-permute-start.10 = (bf16[6,30,32]{2,1,0:T(8,128)(2,1)S(1)}, bf16[6,30,32]{2,1,0:T(8,128)(2,1)S(1)}, u32[]{:S(2)}, u32[]{:S(2)}) collective-permute-start(bf16[6,30,32]{2,1,0:T(8,128)(2,1)S(1)} %pad_maximum_fusion.10), channel_id=1, source_target_pairs={{0,8},{4,12},{8,16},{12,20},{16,24},{20,28},{24,32},{28,36},{32,40... | collective-permute-start | bytes 34568 | tf_op jit(solution)/shard_map/ppermute | solution.py:10
  287.1 19.0 %collective-permute-start.13 = (bf16[6,30,32]{2,1,0:T(8,128)(2,1)S(1)}, bf16[6,30,32]{2,1,0:T(8,128)(2,1)S(1)}, u32[]{:S(2)}, u32[]{:S(2)}) collective-permute-start(bf16[6,30,32]{2,1,0:T(8,128)(2,1)S(1)} %pad_maximum_fusion.10), channel_id=1, source_target_pairs={{8,0},{12,4},{16,8},{20,12},{24,16},{28,20},{32,24},{36,28},{40,32... | collective-permute-start | bytes 34568 | tf_op jit(solution)/shard_map/ppermute | solution.py:10
  290.2 15.8 %collective-permute-start.12 = (bf16[6,30,32]{2,1,0:T(8,128)(2,1)S(1)}, bf16[6,30,32]{2,1,0:T(8,128)(2,1)S(1)}, u32[]{:S(2)}, u32[]{:S(2)}) collective-permute-start(bf16[6,30,32]{2,1,0:T(8,128)(2,1)S(1)} %pad_maximum_fusion.10), channel_id=1, source_target_pairs={{4,0},{8,4},{12,8},{16,12},{20,16},{24,20},{28,24},{32,28},{36,32}... | collective-permute-start | bytes 34568 | tf_op jit(solution)/shard_map/ppermute | solution.py:10
  298.4 7.6 %collective-permute-start.11 = (bf16[6,30,32]{2,1,0:T(8,128)(2,1)S(1)}, bf16[6,30,32]{2,1,0:T(8,128)(2,1)S(1)}, u32[]{:S(2)}, u32[]{:S(2)}) collective-permute-start(bf16[6,30,32]{2,1,0:T(8,128)(2,1)S(1)} %pad_maximum_fusion.10), channel_id=1, source_target_pairs={{0,4},{4,8},{8,12},{12,16},{16,20},{20,24},{24,28},{28,32},{32,36}... | collective-permute-start | bytes 34568 | tf_op jit(solution)/shard_map/ppermute | solution.py:10
  326.2 10.4 %collective-permute-start.14 = (f32[1,16,32]{2,0,1:T(1,128)S(1)}, f32[1,16,32]{2,0,1:T(1,128)S(1)}, u32[]{:S(2)}, u32[]{:S(2)}) collective-permute-start(f32[1,16,32]{2,0,1:T(1,128)S(1)} %bitcast.252), channel_id=1, source_target_pairs={{4,0},{8,4},{12,8},{16,12},{20,16},{24,20},{28,24},{32,28},{36,32}... | collective-permute-start | bytes 6152 | tf_op jit(solution)/shard_map/ppermute | solution.py:10
  336.7 27.3 %collective-permute-start.15 = (f32[7,1,32]{2,0,1:T(8,128)S(1)}, f32[7,1,32]{2,0,1:T(8,128)S(1)}, u32[]{:S(2)}, u32[]{:S(2)}) collective-permute-start(f32[7,1,32]{2,0,1:T(8,128)S(1)} %pad_maximum_fusion.12), channel_id=1, source_target_pairs={{1,0},{2,1},{3,2},{5,4},{6,5},{7,6},{9,8},{10,9},{11,10},{13,12},{... | collective-permute-start | bytes 2696 | tf_op jit(solution)/shard_map/ppermute | solution.py:10
  365.2 13.4 %copy-start.9 = (f32[768,256]{1,0:T(8,128)S(1)}, f32[768,256]{1,0:T(8,128)}, u32[]{:S(2)}) copy-start(f32[768,256]{1,0:T(8,128)} %custom-call) | copy-start | bytes 2359300
  365.2 10.3 %collective-permute-start.16 = (f32[1,32,64]{2,1,0:T(8,128)S(1)}, f32[1,32,64]{2,1,0:T(8,128)S(1)}, u32[]{:S(2)}, u32[]{:S(2)}) collective-permute-start(f32[1,32,64]{2,1,0:T(8,128)S(1)} %slice.435), channel_id=1, source_target_pairs={{4,0},{8,4},{12,8},{16,12},{20,16},{24,20},{28,24},{32,28},{36,32}... | collective-permute-start | bytes 24584 | tf_op jit(solution)/shard_map/ppermute | solution.py:10
  375.6 76.2 %collective-permute-start.17 = (f32[13,1,64]{2,1,0:T(1,128)S(1)}, f32[13,1,64]{2,1,0:T(1,128)S(1)}, u32[]{:S(2)}, u32[]{:S(2)}) collective-permute-start(f32[13,1,64]{2,1,0:T(1,128)S(1)} %pad_maximum_fusion.11), channel_id=1, source_target_pairs={{1,0},{2,1},{3,2},{5,4},{6,5},{7,6},{9,8},{10,9},{11,10},{13,12},{... | collective-permute-start | bytes 9992 | tf_op jit(solution)/shard_map/ppermute | solution.py:10
  452.7 3.7 copy-start.1
where the time goes:
time: 462 us; the launch traced here: 456 us
  local copies, waits for them, and re-layouts  260 us (56%)
  matrix products  106 us (23%)
  starting transfers between devices  68.7 us (15%)
  waiting for transfers between devices  11.9 us (3%)
  other arithmetic  7.13 us (2%)
    dot_general x45, matrix products, accumulate(): return total + jnp.dot(window, weights, preferred_element_type=jnp.float32)  74 us
    unnamed x80, local copies, waits for them, and re-layouts  73.2 us
    reshape x2, local copies, waits for them, and re-layouts, correlate(): weights_all.reshape(15, span_width * layer_count, tile_width * layer_count)  51.4 us
    transpose x2, local copies, waits for them, and re-layouts, correlate(): weights_all = jnp.einsum('abwz,bji->ajwiz', partial_z, pick_y)  41.6 us
    dynamic_slice x30, local copies, waits for them, and re-layouts, accumulate(): window = lax.dynamic_slice_in_dim(stacked, offset_x, row_count, 0)  35.1 us
    slice x56, local copies, waits for them, and re-layouts, correlate(): lax.slice_in_dim(extended, column, column + tile_width * (block_count - 1...  34.3 us
    ppermute x8, starting transfers between devices, from_behind(): return lax.ppermute(value, axis, pairs)  33.7 us
    dot_general x3, matrix products, correlate(): weights_all = jnp.einsum('abwz,bji->ajwiz', partial_z, pick_y)  31.7 us
  transfers between devices with their start and end apart: 18, of which 4 were waited for; matrix products, arithmetic and copies ran while one was open for 67% of the time, Pallas kernels for 0%

commit v1 on v0

v1 whole, which is shorter than its diff:
```python
import functools

import jax
import jax.numpy as jnp
from jax import lax
from jax.experimental import pallas as pl
from jax.experimental.pallas import tpu as pltpu
from jax.sharding import PartitionSpec as P

MESH = pl.DeviceIdType.MESH
BF, F32 = jnp.bfloat16, jnp.float32

BANDS = ((0, 7, 15), (0, 15, 7), (1, 23, 0), (9, 24, 0), (17, 24, 0))
PAIRS = ((1, 2), (0, 3))
MID_WINDOWS = (0, 2, 1, 3)

ROUND1 = (
    ("x_near", (1, 0)),
    ("y_hi", (0, 1)),
    ("c_hh", (1, 1)),
    ("y_lo", (0, -1)),
    ("x_far", (1, 0)),
    ("x_lo", (-1, 0)),
    ("c_hl", (1, -1)),
    ("c_lh", (-1, 1)),
    ("c_ll", (-1, -1)),
)
MIDS = tuple((dx, dy) for dx in (-1, 0, 1) for dy in (-1, 0, 1) if (dx, dy) != (0, 0))
TOPS = tuple(
    (dx, dy) for dx in (-1, 1, -2, 2, 0) for dy in (0, -1, 1) if (dx, dy) != (0, 0)
)


def iota(shape, dim):
    return lax.broadcasted_iota(jnp.int32, shape, dim)


def dot(a, b):
    return jnp.dot(a, b, preferred_element_type=F32)


def near(twice, other):
    gap = jnp.abs(twice - 2 * other)
    return jnp.where(gap == 0, 1.0, jnp.where(gap == 1, 0.5, 0.0)).astype(F32)


def split(value):
    high = value.astype(BF)
    return high, (value - high.astype(F32)).astype(BF)


def roll(value, shift):
    size = value.shape[-1]
    return value if shift % size == 0 else pltpu.roll(value, shift % size, axis=value.ndim - 1)


def toeplitz_chunks(row):
    block = pltpu.roll(
        jnp.broadcast_to(row, (16, 512)), 1, axis=1, stride=1, stride_axis=0
    )
    block = jnp.concatenate([jnp.zeros((16, 128), F32), block], axis=1)
    return [roll(block, -32 * q).astype(BF) for q in range(4)]


def place(chunks, shift, m):
    q = (-shift) % 4
    n = m + 1 + (-shift - q) // 4
    if 0 <= n <= 4:
        return chunks[q][:, 128 * n : 128 * n + 128]
    return jnp.zeros((16, 128), BF)


def kernel(
    count_x, count_y,
    charges, k_fine, k_mid, k_top, out,
    own, edge, xl, xr, yl, yr, corner,
    mid_pack, mid_edge, mxl, mxr, myl, myr, mid_corner,
    top_pack, top_in,
    taps_in, taps, u_fine, u_mid, u_top, shifted, acc, mid_acc, top_acc,
    rows_mid, rows_top, zx, pxy, pz,
    send_sem, recv_sem,
):
    gx, gy = lax.axis_index("gx"), lax.axis_index("gy")

    def valid(dx, dy):
        ok = jnp.bool_(True)
        if dx:
            ok = (gx + dx >= 0) & (gx + dx < count_x)
        if dy:
            ok = ok & (gy + dy >= 0) & (gy + dy < count_y)
        return ok

    for ref in (xl, xr, yl, yr, corner, mxl, mxr, myl, myr, mid_corner, top_in):
        ref[...] = jnp.zeros_like(ref)
    barrier = pltpu.get_barrier_semaphore()
    for dx, dy in TOPS:

        @pl.when(valid(dx, dy))
        def _(dx=dx, dy=dy):
            pl.semaphore_signal(
                barrier, inc=1, device_id=(gx + dx, gy + dy), device_id_type=MESH
            )

    own[...] = charges[...].astype(BF)
    edge[0] = charges[:, 0:8, :].reshape(12, 16, 128).astype(BF)
    edge[1] = charges[:, 56:64, :].reshape(12, 16, 128).astype(BF)

    taps_in[...] = jnp.zeros_like(taps_in)
    for level, ref in enumerate((k_fine, k_mid, k_top)):
        taps_in[level, :, 0:15, 0:15] = ref[...].astype(F32)
    flat = sum(roll(taps_in[level], 16 * level + 1) for level in range(3))
    flat = flat.reshape(240, 128).astype(BF)
    lane_of = iota((240, 512), 0)
    lane_of = (lane_of // 16) * 32 + lane_of % 16
    spread = jnp.where(lane_of == iota((240, 512), 1), 1.0, 0.0).astype(BF)
    taps[...] = lax.dot_general(
        flat, spread, (((0,), (0,)), ((), ())), preferred_element_type=F32
    )[0:48]

    def fine_weights(step, _):
        chunks = toeplitz_chunks(taps[pl.ds(step, 1), :])
        for r in range(22):
            for m in range(2):
                u_fine[step, 16 * r : 16 * r + 16, 128 * m : 128 * m + 128] = place(
                    chunks, r - 14, m
                )
        return 0

    lax.fori_loop(0, 16, fine_weights, 0)

    messages = {
        "x_near": (own.at[20:24], xl.at[4:8]),
        "x_far": (own.at[17:20], xl.at[1:4]),
        "x_lo": (own.at[0:7], xr.at[0:7]),
        "y_hi": (edge.at[1], yl),
        "y_lo": (edge.at[0], yr),
        "c_hh": (edge.at[1, 8:12], corner.at[0]),
        "c_hl": (edge.at[0, 8:12], corner.at[1]),
        "c_lh": (edge.at[1, 0:4], corner.at[2]),
        "c_ll": (edge.at[0, 0:4], corner.at[3]),
    }
    copies = {}

    def describe(key, source, target, direction):
        dx, dy = direction
        n = len(copies)
        copies[key] = (
            pltpu.make_async_remote_copy(
                src_ref=source,
                dst_ref=target,
                send_sem=send_sem.at[n],
                recv_sem=recv_sem.at[n],
                device_id=(gx + dx, gy + dy),
                device_id_type=MESH,
            ),
            direction,
        )

    def start(key):
        copy, (dx, dy) = copies[key]

        @pl.when(valid(dx, dy))
        def _():
            copy.start()

    def arrived(key):
        copy, (dx, dy) = copies[key]

        @pl.when(valid(-dx, -dy))
        def _():
            copy.wait_recv()

    def sent(key):
        copy, (dx, dy) = copies[key]

        @pl.when(valid(dx, dy))
        def _():
            copy.wait_send()

    for key, direction in ROUND1:
        describe(key, *messages[key], direction)

    in_x = 1 + jnp.minimum(gx, 2) + jnp.minimum(count_x - 1 - gx, 2)
    in_y = 1 + jnp.minimum(gy, 1) + jnp.minimum(count_y - 1 - gy, 1)
    pl.semaphore_wait(barrier, in_x * in_y - 1)
    for key, _ in ROUND1:
        start(key)

    def shift_rows(value, x, y0):
        rows = value.shape[0]
        lane = iota((rows, 128), 1)
        for c in range(4):
            turned = roll(value, -c)
            inside = lane + c < 128
            ahead = jnp.where(inside, turned, 0.0) if c else turned
            behind = jnp.where((lane < 124) | (lane + c >= 128), turned, 0.0)
            shifted[1, c, x, y0 : y0 + rows, :] = ahead.astype(BF)
            shifted[0, c, x, y0 : y0 + rows, :] = behind.astype(BF)

    def fine_products(p, groups):
        def body(s, _):
            side = s // 2
            for k in groups:
                lo, hi, first = BANDS[k]
                rows = 16 * (hi - lo)
                left = jnp.concatenate(
                    [u_fine[4 * s + c, 16 * first : 16 * first + rows, :] for c in range(4)],
                    axis=1,
                )
                right = jnp.concatenate(
                    [
                        jnp.concatenate(
                            [
                                shifted[
                                    side, c, 8 * k : 8 * k + 8, 16 * t : 16 * t + 32, :
                                ].reshape(256, 128)
                                for t in PAIRS[p]
                            ],
                            axis=1,
                        )
                        for c in range(4)
                    ],
                    axis=0,
                )
                acc[s, p, 16 * lo : 16 * hi, :] += dot(left, right)
            return 0

        lax.fori_loop(0, 4, body, 0)

    acc[...] = jnp.zeros_like(acc)

    def inner_rows(x, _):
        shift_rows(charges[x, 8:56, :], x + 8, 16)
        return 0

    lax.fori_loop(0, 24, inner_rows, 0)
    fine_products(0, (1, 2, 3))

    def coarse_weights(step, _):
        chunks = toeplitz_chunks(taps[pl.ds(17 + step, 1), :])
        for i in range(13):
            for m in range(7):
                u_mid[step, 16 * i : 16 * i + 16, 128 * m : 128 * m + 128] = place(
                    chunks, i + 1, m
                )
        chunks = toeplitz_chunks(taps[pl.ds(33 + step, 1), :])
        for i in range(8):
            for m in range(6):
                u_top[step, 16 * i : 16 * i + 16, 128 * m : 128 * m + 128] = place(
                    chunks, i + 1, m
                )
        return 0

    lax.fori_loop(0, 15, coarse_weights, 0)

    r, c = iota((384, 256), 0), iota((384, 256), 1)
    pxy[...] = (near(r // 16, c // 16) * near(r % 16, c % 16)).astype(BF)
    for p in range(2):
        r, c = iota((256, 256), 0), iota((256, 256), 1)
        block = r // 64
        block = jnp.where(block == 1, 2, jnp.where(block == 2, 1, block))
        window = jnp.where(c < 128, PAIRS[p][0], PAIRS[p][1])
        pz[p] = jnp.where(block == window, near(c % 128, r % 64), 0.0).astype(BF)

    for key in ("x_near", "y_hi", "c_hh"):
        arrived(key)
    r, c = iota((128, 128), 0), iota((128, 128), 1)
    halve = near(r, c % 64).astype(BF)
    quarter = jnp.where(r < 64, near(r, c % 32), 0.0).astype(BF)
    side_rows = yl[...].astype(F32).reshape(24, 8, 128)
    body = jnp.concatenate([side_rows, charges[...]], axis=1).reshape(24 * 72, 128)
    zx[4:28] = dot(body.astype(BF), halve).reshape(24, 72, 128)
    side_rows = corner[0].astype(F32).reshape(8, 8, 128)[4:8]
    body = jnp.concatenate([side_rows, xl[4:8].astype(F32)], axis=1).reshape(4 * 72, 128)
    zx[0:4] = dot(body.astype(BF), halve).reshape(4, 72, 128)
    rows_mid[:, 0:16, :] = jnp.zeros((13, 16, 128), F32)
    for i in range(13):
        rows_mid[i, 16:88, :] = (
            0.5 * zx[2 * i + 1] + zx[2 * i + 2] + 0.5 * zx[2 * i + 3]
        )
    mid = (
        0.5 * rows_mid[:, pl.ds(7, 40, 2), :]
        + rows_mid[:, pl.ds(8, 40, 2), :]
        + 0.5 * rows_mid[:, pl.ds(9, 40, 2), :]
    ).astype(BF)
    mid_rows = mid.astype(F32)
    lane = iota((12, 16, 128), 2)
    packed = jnp.where(lane < 64, mid_rows[1:13, 8:24], mid_rows[1:13, 24:40])
    mid_pack[...] = packed.astype(BF)
    mid_edge[0] = packed[:, 0:8].reshape(6, 16, 128).astype(BF)
    mid_edge[1] = packed[:, 8:16].reshape(6, 16, 128).astype(BF)

    mid_messages = {
        (1, 0): (mid_pack.at[5:12], mxl.at[1:8]),
        (-1, 0): (mid_pack.at[0:8], mxr),
        (0, 1): (mid_edge.at[1], myl),
        (0, -1): (mid_edge.at[0], myr),
        (1, 1): (mid_edge.at[1, 2:6], mid_corner.at[0]),
        (1, -1): (mid_edge.at[0, 2:6], mid_corner.at[1]),
        (-1, 1): (mid_edge.at[1, 0:4], mid_corner.at[2]),
        (-1, -1): (mid_edge.at[0, 0:4], mid_corner.at[3]),
    }
    for direction in MIDS:
        describe(("mid", direction), *mid_messages[direction], direction)
        start(("mid", direction))

    zt = dot(mid_rows.reshape(520, 128).astype(BF), quarter).reshape(13, 40, 128)
    for i in range(6):
        rows_top[i] = 0.5 * zt[2 * i] + zt[2 * i + 1] + 0.5 * zt[2 * i + 2]
    top = (
        0.5 * rows_top[:, pl.ds(7, 16, 2), :]
        + rows_top[:, pl.ds(8, 16, 2), :]
        + 0.5 * rows_top[:, pl.ds(9, 16, 2), :]
    )
    lane = iota((6, 8, 128), 2)
    packed = jnp.where(lane % 64 < 32, top[:, 0:8], top[:, 8:16])
    top_pack[...] = packed.reshape(3, 16, 128).astype(BF)
    for direction in TOPS:
        dx, dy = direction
        part = {2: slice(2, 3), -2: slice(0, 1)}.get(dx, slice(0, 3))
        target = top_in.at[2 - dx, 1 - dy, part]
        describe(("top", direction), top_pack.at[part], target, direction)
        start(("top", direction))

    arrived("y_lo")

    def outer_columns(n, _):
        low, high = yl[n].astype(F32), yr[n].astype(F32)
        for h in range(2):
            x = 2 * n + h
            shift_rows(
                jnp.concatenate([low[8 * h : 8 * h + 8], charges[x, 0:8, :]], axis=0),
                x + 8,
                0,
            )
            shift_rows(
                jnp.concatenate([charges[x, 56:64, :], high[8 * h : 8 * h + 8]], axis=0),
                x + 8,
                64,
            )
        return 0

    lax.fori_loop(0, 12, outer_columns, 0)
    fine_products(1, (1, 2, 3))

    for key in ("x_far", "x_lo", "c_hl", "c_lh", "c_ll"):
        arrived(key)

    def outer_rows(n, _):
        for side, rows in ((0, xl), (1, xr)):
            low = corner[2 * side, n].astype(F32)
            high = corner[2 * side + 1, n].astype(F32)
            for h in range(2):
                x = 2 * n + h
                shift_rows(
                    jnp.concatenate(
                        [
                            low[8 * h : 8 * h + 8],
                            rows[x].astype(F32),
                            high[8 * h : 8 * h + 8],
                        ],
                        axis=0,
                    ),
                    x + 32 * side,
                    0,
                )
        return 0

    lax.fori_loop(0, 4, outer_rows, 0)
    fine_products(0, (0, 4))
    fine_products(1, (0, 4))

    for direction in MIDS:
        arrived(("mid", direction))
    centre = jnp.concatenate(
        [mxl[...].astype(F32), mid_pack[...].astype(F32), mxr[...].astype(F32)], axis=0
    )

    def column(first, middle, last):
        return jnp.concatenate(
            [
                first.astype(F32).reshape(8, 8, 128),
                middle.astype(F32).reshape(12, 8, 128),
                last.astype(F32).reshape(8, 8, 128),
            ],
            axis=0,
        )

    low = column(mid_corner[0], myl[...], mid_corner[2])
    high = column(mid_corner[1], myr[...], mid_corner[3])
    lane = iota((28, 8, 128), 2)
    low = roll(jnp.where(lane < 64, centre[:, 8:16], low), 64)
    high = roll(jnp.where(lane < 64, high, centre[:, 0:8]), 64)
    field = jnp.concatenate([low, centre, high], axis=1).reshape(896, 128).astype(BF)

    for direction in TOPS:
        arrived(("top", direction))

    def strip(dy):
        parts = []
        for dx in (-2, -1, 0, 1, 2):
            if dx == 0 and dy == 0:
                value = top_pack[...]
            elif dx == -2:
                value = top_in[0, 1 + dy, 2:3]
            elif dx == 2:
                value = top_in[4, 1 + dy, 0:1]
            else:
                value = top_in[2 + dx, 1 + dy]
            parts.append(value.astype(F32).reshape(2 * value.shape[0], 8, 128))
        return jnp.concatenate(parts, axis=0)

    centre, low, high = strip(0), strip(-1), strip(1)
    lane = iota((22, 8, 128), 2) % 64
    low = roll(jnp.where(lane < 32, centre, low), 32)
    high = roll(jnp.where(lane < 32, high, centre), 32)
    top_field = jnp.concatenate([low, centre, high], axis=1).reshape(528, 128).astype(BF)

    mid_acc[...] = jnp.zeros_like(mid_acc)
    top_acc[...] = jnp.zeros_like(top_acc)
    r, c = iota((128, 128), 0), iota((128, 128), 1)

    def coarse_products(step, _):
        hit = r == c + (step - 7)
        move = jnp.where(hit & (r // 64 == c // 64), 1.0, 0.0).astype(BF)
        moved = dot(field, move).reshape(28, 32, 128)
        right = jnp.concatenate(
            [
                moved,
                jnp.concatenate([moved[:, 8:32], moved[:, 0:8]], axis=1),
            ],
            axis=2,
        )
        mid_acc[0:208] += dot(u_mid[step], right.reshape(896, 256).astype(BF))
        move = jnp.where(hit & (r // 32 == c // 32), 1.0, 0.0).astype(BF)
        moved = dot(top_field, move).reshape(22, 24, 128)
        right = jnp.concatenate([moved, jnp.zeros((22, 8, 128), F32)], axis=1)
        right = jnp.concatenate([right.reshape(704, 128), jnp.zeros((64, 128), F32)], axis=0)
        top_acc[...] += dot(u_top[step], right.astype(BF))
        return 0

    lax.fori_loop(0, 15, coarse_products, 0)

    last_x, last_y = gx == count_x - 1, gy == count_y - 1
    r, c = iota((128, 128), 0), iota((128, 128), 1)
    beyond = (last_x & (r // 16 == 6)) | (last_y & (r % 16 == 8) & (c % 64 >= 32))
    high, low = split(jnp.where(beyond, 0.0, top_acc[...]))
    stretch = jnp.where(
        (r < 64) & (r // 32 == c // 64), near(c % 64, r % 32), 0.0
    ).astype(BF)
    wide = dot(
        jnp.concatenate([high, low], axis=1), jnp.concatenate([stretch, stretch], axis=0)
    )
    wide = jnp.concatenate(split(wide), axis=0)
    r, c = iota((208, 128), 0), iota((208, 128), 1)
    along_x = near(r // 16, c // 16)
    parts = []
    for parity in range(2):
        weights = (along_x * near(8 * parity + r % 16, c % 16)).astype(BF)
        parts.append(dot(jnp.concatenate([weights, weights], axis=1), wide))
    mid_u = mid_acc[0:208] + jnp.concatenate(parts, axis=1)

    r, c = iota((208, 256), 0), iota((208, 256), 1)
    beyond = (last_x & (r // 16 == 12)) | (last_y & (r % 16 == 8) & (c >= 192))
    mid_u = jnp.concatenate(split(jnp.where(beyond, 0.0, mid_u)), axis=1)
    weights = jnp.concatenate([pxy[...], pxy[...]], axis=1)
    lane = iota((384, 128), 1)
    for p in range(2):
        wide = dot(mid_u, jnp.concatenate([pz[p], pz[p]], axis=0))
        high, low = split(jnp.concatenate([wide, jnp.zeros((48, 256), F32)], axis=0))
        total = dot(weights, jnp.concatenate([high, low], axis=0))
        for h in range(2):
            lanes = slice(128 * h, 128 * h + 128)
            value = total[:, lanes] + acc[2, p, :, lanes]
            value += jnp.where(lane < 124, roll(acc[3, p, :, lanes], -4), 0.0)
            value += roll(acc[1, p, :, lanes], 4)
            value += jnp.where(lane >= 4, roll(acc[0, p, :, lanes], 8), 0.0)
            t = PAIRS[p][h]
            out[:, 16 * t : 16 * t + 16, :] = value.reshape(24, 16, 128)

    for key in copies:
        sent(key)


def solution(mesh):
    count_x, count_y = mesh.shape["gx"], mesh.shape["gy"]
    vmem = pl.BlockSpec(memory_space=pltpu.VMEM)
    messages = len(ROUND1) + len(MIDS) + len(TOPS)

    def shards(charges, kernel_fine, kernel_mid, kernel_top):
        return pl.pallas_call(
            functools.partial(kernel, count_x, count_y),
            out_shape=jax.ShapeDtypeStruct(charges.shape, F32),
            in_specs=[vmem] * 4,
            out_specs=vmem,
            scratch_shapes=[
                pltpu.VMEM((24, 64, 128), BF),
                pltpu.VMEM((2, 12, 16, 128), BF),
                pltpu.VMEM((8, 64, 128), BF),
                pltpu.VMEM((8, 64, 128), BF),
                pltpu.VMEM((12, 16, 128), BF),
                pltpu.VMEM((12, 16, 128), BF),
                pltpu.VMEM((4, 4, 16, 128), BF),
                pltpu.VMEM((12, 16, 128), BF),
                pltpu.VMEM((2, 6, 16, 128), BF),
                pltpu.VMEM((8, 16, 128), BF),
                pltpu.VMEM((8, 16, 128), BF),
                pltpu.VMEM((6, 16, 128), BF),
                pltpu.VMEM((6, 16, 128), BF),
                pltpu.VMEM((4, 4, 16, 128), BF),
                pltpu.VMEM((3, 16, 128), BF),
                pltpu.VMEM((5, 3, 3, 16, 128), BF),
                pltpu.VMEM((3, 15, 16, 128), F32),
                pltpu.VMEM((48, 512), F32),
                pltpu.VMEM((16, 352, 256), BF),
                pltpu.VMEM((15, 208, 896), BF),
                pltpu.VMEM((15, 128, 768), BF),
                pltpu.VMEM((2, 4, 40, 80, 128), BF),
                pltpu.VMEM((4, 2, 384, 256), F32),
                pltpu.VMEM((208, 256), F32),
                pltpu.VMEM((128, 128), F32),
                pltpu.VMEM((13, 88, 128), F32),
                pltpu.VMEM((6, 40, 128), F32),
                pltpu.VMEM((28, 72, 128), F32),
                pltpu.VMEM((384, 256), BF),
                pltpu.VMEM((2, 256, 256), BF),
                pltpu.SemaphoreType.DMA((messages,)),
                pltpu.SemaphoreType.DMA((messages,)),
            ],
            compiler_params=pltpu.CompilerParams(
                collective_id=0, has_side_effects=True, vmem_limit_bytes=56 * 2**20
            ),
        )(charges, kernel_fine, kernel_mid, kernel_top)

    placed = (P("gx", "gy", None), P(), P(), P())
    return jax.shard_map(
        shards, mesh=mesh, in_specs=placed, out_specs=P("gx", "gy", None), check_vma=False
    )
```

time: 462 us -> 36 us (0.08)
  the two profiles are of different devices: /device:TPU:127 before, /device:TPU:192 now
where the time goes in v1:
time: 36 us; the launch traced here: 35.5 us
  Pallas kernels  33.4 us (93%)
  local copies, waits for them, and re-layouts  2.09 us (6%)
    pallas_call x1, Pallas kernels, shards(): pl.pallas_call(functools.partial(kernel, count_x, count_y), out_shape=jax...  33.4 us
    unnamed x1, local copies, waits for them, and re-layouts  2.09 us

profile of v1, /device:TPU:192, one launch (start us, length us, event | category | flops | bytes accessed | tf_op | source)
XLA Modules:
  0.0 35.5 jit_solution(3018858348426711280)
XLA Ops:
  0.0 33.4 %shard_map.46 = f32[24,64,128]{2,1,0:T(8,128)} custom-call(f32[24,64,128]{2,1,0:T(8,128)} %charges.1, bf16[15,15,15]{2,1,0:T(8,128)(2,1)} %k_fine.1, bf16[15,15,15]{2,1,0:T(8,128)(2,1)} %k_mid.1, bf16[15,15,15]{2,1,0:T(8,128)(2,1)} %k_top.1), custom_call_target="tpu_custom_call" | custom-call | tf_op jit(solution)/shard_map/pallas_call | solution.py:491
  33.4 2.1 %copy.6 = f32[24,64,128]{2,1,0:T(8,128)} copy(f32[24,64,128]{2,1,0:T(8,128)} %shard_map.46) | data formatting | bytes 1572864

commit v2 on v1

--- a/solution.py
+++ b/solution.py
@@ -59,26 +59,57 @@
         jnp.broadcast_to(row, (16, 512)), 1, axis=1, stride=1, stride_axis=0
     )
     block = jnp.concatenate([jnp.zeros((16, 128), F32), block], axis=1)
-    return [roll(block, -32 * q).astype(BF) for q in range(4)]
-
-
-def place(chunks, shift, m):
+    return jnp.concatenate([roll(block, -32 * q).astype(BF) for q in range(4)], axis=1)
+
+
+def place(chunks, index, shift, m):
     q = (-shift) % 4
     n = m + 1 + (-shift - q) // 4
     if 0 <= n <= 4:
-        return chunks[q][:, 128 * n : 128 * n + 128]
+        return chunks[index, :, 640 * q + 128 * n : 640 * q + 128 * n + 128]
     return jnp.zeros((16, 128), BF)
+
+
+def weights(chunks, indices, shifts, lanes):
+    return jnp.concatenate(
+        [
+            jnp.concatenate(
+                [place(chunks, i, shift, m) for i in indices for m in range(lanes // 128)],
+                axis=1,
+            )
+            for shift in shifts
+        ],
+        axis=0,
+    )
+
+
+def moves(c, size):
+    r, l = iota((128, 128), 0), iota((128, 128), 1)
+    at = l % size
+    ahead = (r == l + c) & (at + c < size)
+    behind = ((r == l + c) & (at < size - 4)) | ((r == l + c - size) & (at + c >= size))
+    return jnp.concatenate(
+        [jnp.where(behind, 1.0, 0.0), jnp.where(ahead, 1.0, 0.0)], axis=1
+    ).astype(BF)
+
+
+def gather(parts, size):
+    at = iota(parts[0].shape, 1) % size
+    value = parts[2] + jnp.where(at < size - 4, roll(parts[3], -4), 0.0)
+    value += jnp.where(at >= 4, roll(parts[1], 4), roll(parts[1], 4 - size))
+    back = jnp.where(at >= 4, roll(parts[0], 8 - size), 0.0)
+    return value + jnp.where(at >= 8, roll(parts[0], 8), back)
 
 
 def kernel(
     count_x, count_y,
-    charges, k_fine, k_mid, k_top, out,
-    own, edge, xl, xr, yl, yr, corner,
+    charges_in, k_fine, k_mid, k_top, out,
+    charges, own, edge, xl, xr, yl, yr, corner,
     mid_pack, mid_edge, mxl, mxr, myl, myr, mid_corner,
     top_pack, top_in,
-    taps_in, taps, u_fine, u_mid, u_top, shifted, acc, mid_acc, top_acc,
+    taps_in, taps, chunks, inner, outer, acc, mid_acc, top_acc, mid_right, top_right,
     rows_mid, rows_top, zx, pxy, pz,
-    send_sem, recv_sem,
+    load_sem, send_sem, recv_sem,
 ):
     gx, gy = lax.axis_index("gx"), lax.axis_index("gy")
 
@@ -90,8 +121,22 @@
             ok = ok & (gy + dy >= 0) & (gy + dy < count_y)
         return ok
 
-    for ref in (xl, xr, yl, yr, corner, mxl, mxr, myl, myr, mid_corner, top_in):
-        ref[...] = jnp.zeros_like(ref)
+    load = pltpu.make_async_copy(charges_in, charges, load_sem)
+    load.start()
+
+    @pl.when((gx < 2) | (gx >= count_x - 2) | (gy == 0) | (gy == count_y - 1))
+    def _():
+        for ref in (yl, yr, corner, mxl, mxr, myl, myr, mid_corner, top_in):
+            ref[...] = jnp.zeros_like(ref)
+
+    for ref, dx in ((xl, -1), (xr, 1)):
+
+        @pl.when(~valid(dx, 0))
+        def _(ref=ref):
+            ref[...] = jnp.zeros_like(ref)
+
+    for ref in (xl.at[0], xr.at[7], mxl.at[0]):
+        ref[...] = jnp.zeros(ref.shape, BF)
     barrier = pltpu.get_barrier_semaphore()
     for dx, dy in TOPS:
 
@@ -100,10 +145,6 @@
             pl.semaphore_signal(
                 barrier, inc=1, device_id=(gx + dx, gy + dy), device_id_type=MESH
             )
-
-    own[...] = charges[...].astype(BF)
-    edge[0] = charges[:, 0:8, :].reshape(12, 16, 128).astype(BF)
-    edge[1] = charges[:, 56:64, :].reshape(12, 16, 128).astype(BF)
 
     taps_in[...] = jnp.zeros_like(taps_in)
     for level, ref in enumerate((k_fine, k_mid, k_top)):
@@ -117,16 +158,13 @@
         flat, spread, (((0,), (0,)), ((), ())), preferred_element_type=F32
     )[0:48]
 
-    def fine_weights(step, _):
-        chunks = toeplitz_chunks(taps[pl.ds(step, 1), :])
-        for r in range(22):
-            for m in range(2):
-                u_fine[step, 16 * r : 16 * r + 16, 128 * m : 128 * m + 128] = place(
-                    chunks, r - 14, m
-                )
-        return 0
-
-    lax.fori_loop(0, 16, fine_weights, 0)
+    load.wait()
+    own[...] = charges[...].astype(BF)
+    edge[0] = charges[:, 0:8, :].reshape(12, 16, 128).astype(BF)
+    edge[1] = charges[:, 56:64, :].reshape(12, 16, 128).astype(BF)
+
+    def build(row):
+        chunks[row] = toeplitz_chunks(taps[pl.ds(row, 1), :])
 
     messages = {
         "x_near": (own.at[20:24], xl.at[4:8]),
@@ -180,78 +218,71 @@
     for key, direction in ROUND1:
         describe(key, *messages[key], direction)
 
+    def shift_rows(value, x, target):
+        rows = value.shape[0]
+        lane = iota((rows, 128), 1)
+        for c in range(4):
+            turned = roll(value, -c)
+            ahead = jnp.where(lane + c < 128, turned, 0.0) if c else turned
+            behind = jnp.where((lane < 124) | (lane + c >= 128), turned, 0.0)
+            target[1, c, x] = ahead.astype(BF)
+            target[0, c, x] = behind.astype(BF)
+
+    def window(side, c, k, t):
+        group = pl.ds(8 * k, 8)
+        if t == 0:
+            parts = [outer[0, side, c, group], inner[side, c, group, 0:16, :]]
+        elif t == 3:
+            parts = [inner[side, c, group, 32:48, :], outer[1, side, c, group]]
+        else:
+            parts = [inner[side, c, group, 16 * t - 16 : 16 * t + 16, :]]
+        return jnp.concatenate(parts, axis=1).reshape(256, 128)
+
+    def fine_product(s, p, k):
+        lo, hi, first = BANDS[k]
+        left = weights(
+            chunks, [4 * s + c for c in range(4)], range(first - 14, first - 14 + hi - lo), 256
+        )
+        right = jnp.concatenate(
+            [
+                jnp.concatenate([window(s // 2, c, k, t) for t in PAIRS[p]], axis=1)
+                for c in range(4)
+            ],
+            axis=0,
+        )
+        return dot(left, right)
+
+    def fine_centre(s, p):
+        one, two, three = (fine_product(s, p, k) for k in (1, 2, 3))
+        acc[s, p, 0:16] = one[0:16]
+        acc[s, p, 16:144] = one[16:144] + two[0:128]
+        acc[s, p, 144:240] = one[144:240] + two[128:224] + three[0:96]
+        acc[s, p, 240:368] = two[224:352] + three[96:224]
+        acc[s, p, 368:384] = three[224:240]
+
+    def first_steps(n, _):
+        for h in range(2):
+            build(2 * n + h)
+        for h in range(3):
+            x = 3 * n + h
+            shift_rows(charges[x, 8:56, :], x + 8, inner)
+        return 0
+
+    lax.fori_loop(0, 8, first_steps, 0)
+
     in_x = 1 + jnp.minimum(gx, 2) + jnp.minimum(count_x - 1 - gx, 2)
     in_y = 1 + jnp.minimum(gy, 1) + jnp.minimum(count_y - 1 - gy, 1)
     pl.semaphore_wait(barrier, in_x * in_y - 1)
     for key, _ in ROUND1:
         start(key)
 
-    def shift_rows(value, x, y0):
-        rows = value.shape[0]
-        lane = iota((rows, 128), 1)
-        for c in range(4):
-            turned = roll(value, -c)
-            inside = lane + c < 128
-            ahead = jnp.where(inside, turned, 0.0) if c else turned
-            behind = jnp.where((lane < 124) | (lane + c >= 128), turned, 0.0)
-            shifted[1, c, x, y0 : y0 + rows, :] = ahead.astype(BF)
-            shifted[0, c, x, y0 : y0 + rows, :] = behind.astype(BF)
-
-    def fine_products(p, groups):
-        def body(s, _):
-            side = s // 2
-            for k in groups:
-                lo, hi, first = BANDS[k]
-                rows = 16 * (hi - lo)
-                left = jnp.concatenate(
-                    [u_fine[4 * s + c, 16 * first : 16 * first + rows, :] for c in range(4)],
-                    axis=1,
-                )
-                right = jnp.concatenate(
-                    [
-                        jnp.concatenate(
-                            [
-                                shifted[
-                                    side, c, 8 * k : 8 * k + 8, 16 * t : 16 * t + 32, :
-                                ].reshape(256, 128)
-                                for t in PAIRS[p]
-                            ],
-                            axis=1,
-                        )
-                        for c in range(4)
-                    ],
-                    axis=0,
-                )
-                acc[s, p, 16 * lo : 16 * hi, :] += dot(left, right)
-            return 0
-
-        lax.fori_loop(0, 4, body, 0)
-
-    acc[...] = jnp.zeros_like(acc)
-
-    def inner_rows(x, _):
-        shift_rows(charges[x, 8:56, :], x + 8, 16)
-        return 0
-
-    lax.fori_loop(0, 24, inner_rows, 0)
-    fine_products(0, (1, 2, 3))
-
-    def coarse_weights(step, _):
-        chunks = toeplitz_chunks(taps[pl.ds(17 + step, 1), :])
-        for i in range(13):
-            for m in range(7):
-                u_mid[step, 16 * i : 16 * i + 16, 128 * m : 128 * m + 128] = place(
-                    chunks, i + 1, m
-                )
-        chunks = toeplitz_chunks(taps[pl.ds(33 + step, 1), :])
-        for i in range(8):
-            for m in range(6):
-                u_top[step, 16 * i : 16 * i + 16, 128 * m : 128 * m + 128] = place(
-                    chunks, i + 1, m
-                )
-        return 0
-
-    lax.fori_loop(0, 15, coarse_weights, 0)
+    def second_steps(s, _):
+        fine_centre(s, 0)
+        for h in range(8):
+            build(16 + 8 * s + h)
+        return 0
+
+    lax.fori_loop(0, 4, second_steps, 0)
 
     r, c = iota((384, 256), 0), iota((384, 256), 1)
     pxy[...] = (near(r // 16, c // 16) * near(r % 16, c % 16)).astype(BF)
@@ -259,8 +290,8 @@
         r, c = iota((256, 256), 0), iota((256, 256), 1)
         block = r // 64
         block = jnp.where(block == 1, 2, jnp.where(block == 2, 1, block))
-        window = jnp.where(c < 128, PAIRS[p][0], PAIRS[p][1])
-        pz[p] = jnp.where(block == window, near(c % 128, r % 64), 0.0).astype(BF)
+        column_of = jnp.where(c < 128, PAIRS[p][0], PAIRS[p][1])
+        pz[p] = jnp.where(block == column_of, near(c % 128, r % 64), 0.0).astype(BF)
 
     for key in ("x_near", "y_hi", "c_hh"):
         arrived(key)
@@ -331,17 +362,22 @@
             shift_rows(
                 jnp.concatenate([low[8 * h : 8 * h + 8], charges[x, 0:8, :]], axis=0),
                 x + 8,
-                0,
+                outer.at[0],
             )
             shift_rows(
                 jnp.concatenate([charges[x, 56:64, :], high[8 * h : 8 * h + 8]], axis=0),
                 x + 8,
-                64,
+                outer.at[1],
             )
         return 0
 
-    lax.fori_loop(0, 12, outer_columns, 0)
-    fine_products(1, (1, 2, 3))
+    lax.fori_loop(0, 12, outer_columns, 0, unroll=2)
+
+    def third_steps(s, _):
+        fine_centre(s, 1)
+        return 0
+
+    lax.fori_loop(0, 4, third_steps, 0)
 
     for key in ("x_far", "x_lo", "c_hl", "c_lh", "c_ll"):
         arrived(key)
@@ -352,46 +388,74 @@
             high = corner[2 * side + 1, n].astype(F32)
             for h in range(2):
                 x = 2 * n + h
-                shift_rows(
-                    jnp.concatenate(
-                        [
-                            low[8 * h : 8 * h + 8],
-                            rows[x].astype(F32),
-                            high[8 * h : 8 * h + 8],
-                        ],
-                        axis=0,
-                    ),
-                    x + 32 * side,
-                    0,
-                )
+                target = x + 32 * side
+                row = rows[x].astype(F32)
+                part = slice(8 * h, 8 * h + 8)
+                shift_rows(row[8:56], target, inner)
+                shift_rows(jnp.concatenate([low[part], row[0:8]], axis=0), target, outer.at[0])
+                shift_rows(jnp.concatenate([row[56:64], high[part]], axis=0), target, outer.at[1])
         return 0
 
     lax.fori_loop(0, 4, outer_rows, 0)
-    fine_products(0, (0, 4))
-    fine_products(1, (0, 4))
+
+    def fourth_steps(s, _):
+        for p in range(2):
+            for k in (0, 4):
+                lo, hi, _ = BANDS[k]
+                acc[s, p, 16 * lo : 16 * hi, :] += fine_product(s, p, k)
+        return 0
+
+    lax.fori_loop(0, 4, fourth_steps, 0)
+
+    def mid_field(centre, low, high):
+        lane = iota(low.shape, 2)
+        first = roll(jnp.where(lane < 64, centre[:, 8:16], low), 64)
+        last = roll(jnp.where(lane < 64, high, centre[:, 0:8]), 64)
+        field = jnp.concatenate([first, centre, last], axis=1)
+        return field.reshape(32 * field.shape[0], 128).astype(BF)
+
+    def mid_shift(field, start):
+        rows = field.shape[0]
+        for c in range(4):
+            moved = dot(field, moves(c, 64)).reshape(rows // 32, 32, 256)
+            turned = jnp.concatenate([moved[:, 8:32], moved[:, 0:8]], axis=1)
+            for side in range(2):
+                lanes = slice(128 * side, 128 * side + 128)
+                both = jnp.concatenate([moved[:, :, lanes], turned[:, :, lanes]], axis=2)
+                mid_right[side, c, start : start + rows, :] = both.reshape(rows, 256).astype(BF)
+
+    def mid_product(s, blocks, start, rows):
+        left = weights(
+            chunks,
+            [16 + 4 * s + c for c in range(4)],
+            [i + 1 - start // 32 for i in blocks],
+            rows,
+        )
+        right = jnp.concatenate(
+            [mid_right[s // 2, c, start : start + rows, :] for c in range(4)], axis=0
+        )
+        return dot(left, right)
+
+    def pairs(ref):
+        value = ref[...].astype(F32)
+        return value.reshape(2 * value.shape[0], 8, 128)
+
+    for direction in ((0, 1), (0, -1)):
+        arrived(("mid", direction))
+    mid_shift(mid_field(mid_pack[...].astype(F32), pairs(myl), pairs(myr)), 256)
+
+    def fifth_steps(s, _):
+        mid_acc[s] = mid_product(s, range(13), 256, 384)
+        return 0
+
+    lax.fori_loop(0, 4, fifth_steps, 0)
 
     for direction in MIDS:
-        arrived(("mid", direction))
-    centre = jnp.concatenate(
-        [mxl[...].astype(F32), mid_pack[...].astype(F32), mxr[...].astype(F32)], axis=0
-    )
-
-    def column(first, middle, last):
-        return jnp.concatenate(
-            [
-                first.astype(F32).reshape(8, 8, 128),
-                middle.astype(F32).reshape(12, 8, 128),
-                last.astype(F32).reshape(8, 8, 128),
-            ],
-            axis=0,
-        )
-
-    low = column(mid_corner[0], myl[...], mid_corner[2])
-    high = column(mid_corner[1], myr[...], mid_corner[3])
-    lane = iota((28, 8, 128), 2)
-    low = roll(jnp.where(lane < 64, centre[:, 8:16], low), 64)
-    high = roll(jnp.where(lane < 64, high, centre[:, 0:8]), 64)
-    field = jnp.concatenate([low, centre, high], axis=1).reshape(896, 128).astype(BF)
+        if direction[0]:
+            arrived(("mid", direction))
+    for side, rows in ((0, mxl), (1, mxr)):
+        low, high = pairs(mid_corner.at[2 * side]), pairs(mid_corner.at[2 * side + 1])
+        mid_shift(mid_field(rows[...].astype(F32), low, high), 640 * side)
 
     for direction in TOPS:
         arrived(("top", direction))
@@ -400,51 +464,47 @@
         parts = []
         for dx in (-2, -1, 0, 1, 2):
             if dx == 0 and dy == 0:
-                value = top_pack[...]
+                ref = top_pack
             elif dx == -2:
-                value = top_in[0, 1 + dy, 2:3]
+                ref = top_in.at[0, 1 + dy, 2:3]
             elif dx == 2:
-                value = top_in[4, 1 + dy, 0:1]
+                ref = top_in.at[4, 1 + dy, 0:1]
             else:
-                value = top_in[2 + dx, 1 + dy]
-            parts.append(value.astype(F32).reshape(2 * value.shape[0], 8, 128))
+                ref = top_in.at[2 + dx, 1 + dy]
+            parts.append(pairs(ref))
         return jnp.concatenate(parts, axis=0)
 
     centre, low, high = strip(0), strip(-1), strip(1)
     lane = iota((22, 8, 128), 2) % 64
     low = roll(jnp.where(lane < 32, centre, low), 32)
     high = roll(jnp.where(lane < 32, high, centre), 32)
-    top_field = jnp.concatenate([low, centre, high], axis=1).reshape(528, 128).astype(BF)
-
-    mid_acc[...] = jnp.zeros_like(mid_acc)
-    top_acc[...] = jnp.zeros_like(top_acc)
-    r, c = iota((128, 128), 0), iota((128, 128), 1)
-
-    def coarse_products(step, _):
-        hit = r == c + (step - 7)
-        move = jnp.where(hit & (r // 64 == c // 64), 1.0, 0.0).astype(BF)
-        moved = dot(field, move).reshape(28, 32, 128)
-        right = jnp.concatenate(
-            [
-                moved,
-                jnp.concatenate([moved[:, 8:32], moved[:, 0:8]], axis=1),
-            ],
-            axis=2,
-        )
-        mid_acc[0:208] += dot(u_mid[step], right.reshape(896, 256).astype(BF))
-        move = jnp.where(hit & (r // 32 == c // 32), 1.0, 0.0).astype(BF)
-        moved = dot(top_field, move).reshape(22, 24, 128)
-        right = jnp.concatenate([moved, jnp.zeros((22, 8, 128), F32)], axis=1)
-        right = jnp.concatenate([right.reshape(704, 128), jnp.zeros((64, 128), F32)], axis=0)
-        top_acc[...] += dot(u_top[step], right.astype(BF))
-        return 0
-
-    lax.fori_loop(0, 15, coarse_products, 0)
+    field = jnp.concatenate([low, centre, high], axis=1).reshape(528, 128).astype(BF)
+    lane = iota((20, 24, 128), 2)
+    for c in range(4):
+        moved = dot(field, moves(c, 32)).reshape(22, 24, 256)
+        moved = jnp.concatenate([moved, jnp.zeros((2, 24, 256), F32)], axis=0)
+        for side in range(2):
+            part = moved[:, :, 128 * side : 128 * side + 128]
+            both = jnp.where(lane < 64, part[0:20], part[4:24])
+            both = jnp.concatenate([both, jnp.zeros((20, 8, 128), F32)], axis=1)
+            top_right[side, c] = both.reshape(640, 128).astype(BF)
+
+    def sixth_steps(s, _):
+        mid_acc[s, 0:112, :] += mid_product(s, range(7), 0, 256)
+        mid_acc[s, 80:208, :] += mid_product(s, range(5, 13), 640, 256)
+        left = weights(chunks, [32 + 4 * s + c for c in range(4)], range(1, 5), 640)
+        right = jnp.concatenate([top_right[s // 2, c] for c in range(4)], axis=0)
+        top_acc[s] = dot(left, right)
+        return 0
+
+    lax.fori_loop(0, 4, sixth_steps, 0)
 
     last_x, last_y = gx == count_x - 1, gy == count_y - 1
     r, c = iota((128, 128), 0), iota((128, 128), 1)
     beyond = (last_x & (r // 16 == 6)) | (last_y & (r % 16 == 8) & (c % 64 >= 32))
-    high, low = split(jnp.where(beyond, 0.0, top_acc[...]))
+    top_e = gather([top_acc[s] for s in range(4)], 32)
+    top_e = jnp.concatenate([top_e, roll(top_e, 64)], axis=0)
+    high, low = split(jnp.where(beyond, 0.0, top_e))
     stretch = jnp.where(
         (r < 64) & (r // 32 == c // 64), near(c % 64, r % 32), 0.0
     ).astype(BF)
@@ -456,19 +516,19 @@
     along_x = near(r // 16, c // 16)
     parts = []
     for parity in range(2):
-        weights = (along_x * near(8 * parity + r % 16, c % 16)).astype(BF)
-        parts.append(dot(jnp.concatenate([weights, weights], axis=1), wide))
-    mid_u = mid_acc[0:208] + jnp.concatenate(parts, axis=1)
+        spread = (along_x * near(8 * parity + r % 16, c % 16)).astype(BF)
+        parts.append(dot(jnp.concatenate([spread, spread], axis=1), wide))
+    mid_u = gather([mid_acc[s] for s in range(4)], 64) + jnp.concatenate(parts, axis=1)
 
     r, c = iota((208, 256), 0), iota((208, 256), 1)
     beyond = (last_x & (r // 16 == 12)) | (last_y & (r % 16 == 8) & (c >= 192))
     mid_u = jnp.concatenate(split(jnp.where(beyond, 0.0, mid_u)), axis=1)
-    weights = jnp.concatenate([pxy[...], pxy[...]], axis=1)
+    spread = jnp.concatenate([pxy[...], pxy[...]], axis=1)
     lane = iota((384, 128), 1)
     for p in range(2):
         wide = dot(mid_u, jnp.concatenate([pz[p], pz[p]], axis=0))
         high, low = split(jnp.concatenate([wide, jnp.zeros((48, 256), F32)], axis=0))
-        total = dot(weights, jnp.concatenate([high, low], axis=0))
+        total = dot(spread, jnp.concatenate([high, low], axis=0))
         for h in range(2):
             lanes = slice(128 * h, 128 * h + 128)
             value = total[:, lanes] + acc[2, p, :, lanes]
@@ -491,9 +551,10 @@
         return pl.pallas_call(
             functools.partial(kernel, count_x, count_y),
             out_shape=jax.ShapeDtypeStruct(charges.shape, F32),
-            in_specs=[vmem] * 4,
+            in_specs=[pl.BlockSpec(memory_space=pl.ANY)] + [vmem] * 3,
             out_specs=vmem,
             scratch_shapes=[
+                pltpu.VMEM((24, 64, 128), F32),
                 pltpu.VMEM((24, 64, 128), BF),
                 pltpu.VMEM((2, 12, 16, 128), BF),
                 pltpu.VMEM((8, 64, 128), BF),
@@ -512,18 +573,20 @@
                 pltpu.VMEM((5, 3, 3, 16, 128), BF),
                 pltpu.VMEM((3, 15, 16, 128), F32),
                 pltpu.VMEM((48, 512), F32),
-                pltpu.VMEM((16, 352, 256), BF),
-                pltpu.VMEM((15, 208, 896), BF),
-                pltpu.VMEM((15, 128, 768), BF),
-                pltpu.VMEM((2, 4, 40, 80, 128), BF),
+                pltpu.VMEM((48, 16, 2560), BF),
+                pltpu.VMEM((2, 4, 40, 48, 128), BF),
+                pltpu.VMEM((2, 2, 4, 40, 16, 128), BF),
                 pltpu.VMEM((4, 2, 384, 256), F32),
-                pltpu.VMEM((208, 256), F32),
-                pltpu.VMEM((128, 128), F32),
+                pltpu.VMEM((4, 208, 256), F32),
+                pltpu.VMEM((4, 64, 128), F32),
+                pltpu.VMEM((2, 4, 896, 256), BF),
+                pltpu.VMEM((2, 4, 640, 128), BF),
                 pltpu.VMEM((13, 88, 128), F32),
                 pltpu.VMEM((6, 40, 128), F32),
                 pltpu.VMEM((28, 72, 128), F32),
                 pltpu.VMEM((384, 256), BF),
                 pltpu.VMEM((2, 256, 256), BF),
+                pltpu.SemaphoreType.DMA,
                 pltpu.SemaphoreType.DMA((messages,)),
                 pltpu.SemaphoreType.DMA((messages,)),
             ],

time: 36 us -> 28.8 us (0.80)
  Pallas kernels: 33.4 us -> 26.5 us
    pallas_call x1, Pallas kernels: 33.4 us -> 26.5 us  [shards(): pl.pallas_call(functools.partial(kernel, count_x, count_y), out_shape=jax...]
where the time goes in v2:
time: 28.8 us; the launch traced here: 28.6 us
  Pallas kernels  26.5 us (92%)
  local copies, waits for them, and re-layouts  2.09 us (7%)
    pallas_call x1, Pallas kernels, shards(): pl.pallas_call(functools.partial(kernel, count_x, count_y), out_shape=jax...  26.5 us
    unnamed x1, local copies, waits for them, and re-layouts  2.09 us

profile of v2, /device:TPU:192, one launch (start us, length us, event | category | flops | bytes accessed | tf_op | source)
XLA Modules:
  0.0 28.6 jit_solution(8699275923786926195)
XLA Ops:
  0.0 26.5 %shard_map.46 = f32[24,64,128]{2,1,0:T(8,128)} custom-call(f32[24,64,128]{2,1,0:T(8,128)} %charges_in.1, bf16[15,15,15]{2,1,0:T(8,128)(2,1)} %k_fine.1, bf16[15,15,15]{2,1,0:T(8,128)(2,1)} %k_mid.1, bf16[15,15,15]{2,1,0:T(8,128)(2,1)} %k_top.1), custom_call_target="tpu_custom_call" | custom-call | tf_op jit(solution)/shard_map/pallas_call | solution.py:551
  26.5 2.1 %copy.6 = f32[24,64,128]{2,1,0:T(8,128)} copy(f32[24,64,128]{2,1,0:T(8,128)} %shard_map.46) | data formatting | bytes 1572864

commit v3 on v2

--- a/solution.py
+++ b/solution.py
@@ -25,6 +25,8 @@
     ("c_lh", (-1, 1)),
     ("c_ll", (-1, -1)),
 )
+EARLY = ("x_near", "y_hi", "c_hh", "y_lo", "x_far", "x_lo", "c_hl", "c_lh", "c_ll")
+LATE = ()
 MIDS = tuple((dx, dy) for dx in (-1, 0, 1) for dy in (-1, 0, 1) if (dx, dy) != (0, 0))
 TOPS = tuple(
     (dx, dy) for dx in (-1, 1, -2, 2, 0) for dy in (0, -1, 1) if (dx, dy) != (0, 0)
@@ -268,12 +270,13 @@
             shift_rows(charges[x, 8:56, :], x + 8, inner)
         return 0
 
-    lax.fori_loop(0, 8, first_steps, 0)
-
     in_x = 1 + jnp.minimum(gx, 2) + jnp.minimum(count_x - 1 - gx, 2)
     in_y = 1 + jnp.minimum(gy, 1) + jnp.minimum(count_y - 1 - gy, 1)
     pl.semaphore_wait(barrier, in_x * in_y - 1)
-    for key, _ in ROUND1:
+    for key in EARLY:
+        start(key)
+    lax.fori_loop(0, 8, first_steps, 0)
+    for key in LATE:
         start(key)
 
     def second_steps(s, _):
@@ -550,7 +553,7 @@
     def shards(charges, kernel_fine, kernel_mid, kernel_top):
         return pl.pallas_call(
             functools.partial(kernel, count_x, count_y),
-            out_shape=jax.ShapeDtypeStruct(charges.shape, F32),
+            out_shape=pltpu.VMEM(charges.shape, F32),
             in_specs=[pl.BlockSpec(memory_space=pl.ANY)] + [vmem] * 3,
             out_specs=vmem,
             scratch_shapes=[

time: 28.8 us -> 25.6 us (0.89)
  Pallas kernels: 26.5 us -> 24.4 us
  local copies, waits for them, and re-layouts: 2.09 us -> 0.88 us
    pallas_call x1, Pallas kernels: 26.5 us -> 24.4 us  [shards(): pl.pallas_call(functools.partial(kernel, count_x, count_y), out_shape=plt...]
    unnamed x1, local copies, waits for them, and re-layouts: 2.09 us -> 0.88 us
where the time goes in v3:
time: 25.6 us; the launch traced here: 25.3 us
  Pallas kernels  24.4 us (95%)
  local copies, waits for them, and re-layouts  0.88 us (3%)
    pallas_call x1, Pallas kernels, shards(): pl.pallas_call(functools.partial(kernel, count_x, count_y), out_shape=plt...  24.4 us
    unnamed x1, local copies, waits for them, and re-layouts  0.88 us

profile of v3, /device:TPU:192, one launch (start us, length us, event | category | flops | bytes accessed | tf_op | source)
XLA Modules:
  0.0 25.3 jit_solution(9672358829714613333)
XLA Ops:
  0.0 24.4 %shard_map.46 = f32[24,64,128]{2,1,0:T(8,128)S(1)} custom-call(f32[24,64,128]{2,1,0:T(8,128)} %charges_in.1, bf16[15,15,15]{2,1,0:T(8,128)(2,1)} %k_fine.1, bf16[15,15,15]{2,1,0:T(8,128)(2,1)} %k_mid.1, bf16[15,15,15]{2,1,0:T(8,128)(2,1)} %k_top.1), custom_call_target="tpu_custom_call" | custom-call | tf_op jit(solution)/shard_map/pallas_call | solution.py:554
  24.4 0.9 %copy.6 = f32[24,64,128]{2,1,0:T(8,128)} copy(f32[24,64,128]{2,1,0:T(8,128)S(1)} %shard_map.46) | data formatting | bytes 1572864

commit v4 on v3

--- a/solution.py
+++ b/solution.py
@@ -85,6 +85,20 @@
     )
 
 
+def terms(s):
+    return (1, 2, 3) if isinstance(s, int) and s == 0 else (0, 1, 2, 3)
+
+
+def each_sum(body):
+    body(0)
+
+    def step(s, _):
+        body(s)
+        return 0
+
+    lax.fori_loop(1, 4, step, 0)
+
+
 def moves(c, size):
     r, l = iota((128, 128), 0), iota((128, 128), 1)
     at = l % size
@@ -243,12 +257,12 @@
     def fine_product(s, p, k):
         lo, hi, first = BANDS[k]
         left = weights(
-            chunks, [4 * s + c for c in range(4)], range(first - 14, first - 14 + hi - lo), 256
+            chunks, [4 * s + c for c in terms(s)], range(first - 14, first - 14 + hi - lo), 256
         )
         right = jnp.concatenate(
             [
                 jnp.concatenate([window(s // 2, c, k, t) for t in PAIRS[p]], axis=1)
-                for c in range(4)
+                for c in terms(s)
             ],
             axis=0,
         )
@@ -263,12 +277,18 @@
         acc[s, p, 368:384] = three[224:240]
 
     def first_steps(n, _):
-        for h in range(2):
-            build(2 * n + h)
+        build(8 + n)
         for h in range(3):
             x = 3 * n + h
             shift_rows(charges[x, 8:56, :], x + 8, inner)
         return 0
+
+    def fine_weights(n, _):
+        for h in range(4):
+            build(4 * n + h)
+        return 0
+
+    lax.fori_loop(0, 2, fine_weights, 0)
 
     in_x = 1 + jnp.minimum(gx, 2) + jnp.minimum(count_x - 1 - gx, 2)
     in_y = 1 + jnp.minimum(gy, 1) + jnp.minimum(count_y - 1 - gy, 1)
@@ -279,13 +299,12 @@
     for key in LATE:
         start(key)
 
-    def second_steps(s, _):
+    def second_steps(s):
         fine_centre(s, 0)
         for h in range(8):
             build(16 + 8 * s + h)
-        return 0
-
-    lax.fori_loop(0, 4, second_steps, 0)
+
+    each_sum(second_steps)
 
     r, c = iota((384, 256), 0), iota((384, 256), 1)
     pxy[...] = (near(r // 16, c // 16) * near(r % 16, c % 16)).astype(BF)
@@ -376,11 +395,10 @@
 
     lax.fori_loop(0, 12, outer_columns, 0, unroll=2)
 
-    def third_steps(s, _):
+    def third_steps(s):
         fine_centre(s, 1)
-        return 0
-
-    lax.fori_loop(0, 4, third_steps, 0)
+
+    each_sum(third_steps)
 
     for key in ("x_far", "x_lo", "c_hl", "c_lh", "c_ll"):
         arrived(key)
@@ -401,14 +419,13 @@
 
     lax.fori_loop(0, 4, outer_rows, 0)
 
-    def fourth_steps(s, _):
+    def fourth_steps(s):
         for p in range(2):
             for k in (0, 4):
                 lo, hi, _ = BANDS[k]
                 acc[s, p, 16 * lo : 16 * hi, :] += fine_product(s, p, k)
-        return 0
-
-    lax.fori_loop(0, 4, fourth_steps, 0)
+
+    each_sum(fourth_steps)
 
     def mid_field(centre, low, high):
         lane = iota(low.shape, 2)
@@ -430,12 +447,12 @@
     def mid_product(s, blocks, start, rows):
         left = weights(
             chunks,
-            [16 + 4 * s + c for c in range(4)],
+            [16 + 4 * s + c for c in terms(s)],
             [i + 1 - start // 32 for i in blocks],
             rows,
         )
         right = jnp.concatenate(
-            [mid_right[s // 2, c, start : start + rows, :] for c in range(4)], axis=0
+            [mid_right[s // 2, c, start : start + rows, :] for c in terms(s)], axis=0
         )
         return dot(left, right)
 
@@ -447,11 +464,10 @@
         arrived(("mid", direction))
     mid_shift(mid_field(mid_pack[...].astype(F32), pairs(myl), pairs(myr)), 256)
 
-    def fifth_steps(s, _):
+    def fifth_steps(s):
         mid_acc[s] = mid_product(s, range(13), 256, 384)
-        return 0
-
-    lax.fori_loop(0, 4, fifth_steps, 0)
+
+    each_sum(fifth_steps)
 
     for direction in MIDS:
         if direction[0]:
@@ -492,15 +508,14 @@
             both = jnp.concatenate([both, jnp.zeros((20, 8, 128), F32)], axis=1)
             top_right[side, c] = both.reshape(640, 128).astype(BF)
 
-    def sixth_steps(s, _):
+    def sixth_steps(s):
         mid_acc[s, 0:112, :] += mid_product(s, range(7), 0, 256)
         mid_acc[s, 80:208, :] += mid_product(s, range(5, 13), 640, 256)
-        left = weights(chunks, [32 + 4 * s + c for c in range(4)], range(1, 5), 640)
-        right = jnp.concatenate([top_right[s // 2, c] for c in range(4)], axis=0)
+        left = weights(chunks, [32 + 4 * s + c for c in terms(s)], range(1, 5), 640)
+        right = jnp.concatenate([top_right[s // 2, c] for c in terms(s)], axis=0)
         top_acc[s] = dot(left, right)
-        return 0
-
-    lax.fori_loop(0, 4, sixth_steps, 0)
+
+    each_sum(sixth_steps)
 
     last_x, last_y = gx == count_x - 1, gy == count_y - 1
     r, c = iota((128, 128), 0), iota((128, 128), 1)

time: 25.6 us -> 25.5 us (level)
  no operation moved by 1% of the time
where the time goes in v4:
time: 25.5 us; the launch traced here: 25.1 us
  Pallas kernels  24.2 us (95%)
  local copies, waits for them, and re-layouts  0.88 us (3%)
    pallas_call x1, Pallas kernels, shards(): pl.pallas_call(functools.partial(kernel, count_x, count_y), out_shape=plt...  24.2 us
    unnamed x1, local copies, waits for them, and re-layouts  0.88 us

profile of v4, /device:TPU:192, one launch (start us, length us, event | category | flops | bytes accessed | tf_op | source)
XLA Modules:
  0.0 25.1 jit_solution(17594669311684477858)
XLA Ops:
  0.0 24.2 %shard_map.46 = f32[24,64,128]{2,1,0:T(8,128)S(1)} custom-call(f32[24,64,128]{2,1,0:T(8,128)} %charges_in.1, bf16[15,15,15]{2,1,0:T(8,128)(2,1)} %k_fine.1, bf16[15,15,15]{2,1,0:T(8,128)(2,1)} %k_mid.1, bf16[15,15,15]{2,1,0:T(8,128)(2,1)} %k_top.1), custom_call_target="tpu_custom_call" | custom-call | tf_op jit(solution)/shard_map/pallas_call | solution.py:569
  24.2 0.9 %copy.6 = f32[24,64,128]{2,1,0:T(8,128)} copy(f32[24,64,128]{2,1,0:T(8,128)S(1)} %shard_map.46) | data formatting | bytes 1572864

commit v5 on v4

--- a/solution.py
+++ b/solution.py
@@ -89,14 +89,15 @@
     return (1, 2, 3) if isinstance(s, int) and s == 0 else (0, 1, 2, 3)
 
 
-def each_sum(body):
-    body(0)
+def each_sum(body, first=0, last=4):
+    if first == 0:
+        body(0)
 
     def step(s, _):
         body(s)
         return 0
 
-    lax.fori_loop(1, 4, step, 0)
+    lax.fori_loop(max(first, 1), last, step, 0)
 
 
 def moves(c, size):
@@ -304,7 +305,7 @@
         for h in range(8):
             build(16 + 8 * s + h)
 
-    each_sum(second_steps)
+    each_sum(second_steps, 0, 2)
 
     r, c = iota((384, 256), 0), iota((384, 256), 1)
     pxy[...] = (near(r // 16, c // 16) * near(r % 16, c % 16)).astype(BF)
@@ -374,6 +375,8 @@
         target = top_in.at[2 - dx, 1 - dy, part]
         describe(("top", direction), top_pack.at[part], target, direction)
         start(("top", direction))
+
+    each_sum(second_steps, 2, 4)
 
     arrived("y_lo")
 

time: 25.5 us -> 26.5 us (1.039)
  the two profiles are of different devices: /device:TPU:192 before, /device:TPU:129 now
where the time goes in v5:
time: 26.5 us; the launch traced here: 26.4 us
  Pallas kernels  25.5 us (96%)
  local copies, waits for them, and re-layouts  0.88 us (3%)
    pallas_call x1, Pallas kernels, shards(): pl.pallas_call(functools.partial(kernel, count_x, count_y), out_shape=plt...  25.5 us
    unnamed x1, local copies, waits for them, and re-layouts  0.88 us

profile of v5, /device:TPU:129, one launch (start us, length us, event | category | flops | bytes accessed | tf_op | source)
XLA Modules:
  0.0 26.4 jit_solution(9032822329874839533)
XLA Ops:
  0.0 25.5 %shard_map.46 = f32[24,64,128]{2,1,0:T(8,128)S(1)} custom-call(f32[24,64,128]{2,1,0:T(8,128)} %charges_in.1, bf16[15,15,15]{2,1,0:T(8,128)(2,1)} %k_fine.1, bf16[15,15,15]{2,1,0:T(8,128)(2,1)} %k_mid.1, bf16[15,15,15]{2,1,0:T(8,128)(2,1)} %k_top.1), custom_call_target="tpu_custom_call" | custom-call | tf_op jit(solution)/shard_map/pallas_call | solution.py:572
  25.5 0.9 %copy.6 = f32[24,64,128]{2,1,0:T(8,128)} copy(f32[24,64,128]{2,1,0:T(8,128)S(1)} %shard_map.46) | data formatting | bytes 1572864
